TPU v7x, 32 devices: a whole 2x2x4 slice. The times are simulated.
32 devices in a mesh: dp: 2 (over core), ctx: 4 (over y, x), head: 4 (over z).
Axes of the slice: x: 2, y: 2, z: 4, core: 2. Of those that a mesh axis runs over, the one named last changes fastest.
Arguments:
- value_input: bfloat16 [2, 2048, 8192], P('dp', 'ctx', 'head'), may hold values from -6 to 6
- state_proj: bfloat16 [2, 2048, 256], P('dp', 'ctx'), may hold values from -6 to 6
- step_raw: float32 [2, 128, 2048], P('dp', 'head', 'ctx'), may hold values from -4 to 10
- doc_lengths: int32 [2, 8], P('dp'), may hold values from 1 to 1024, 2048 in all within a row
- conv_value: float32 [4, 8192], P(None, 'head'), may hold values from -2 to 2
- conv_state: float32 [4, 256], replicated, may hold values from -2 to 2
- step_bias: float32 [128], P('head'), may hold values from -8 to -3.5
- decay_log: float32 [128], P('head'), may hold values from -1.5 to 1
- skip_gain: float32 [128], P('head'), may hold values from 0.2 to 1
- out_grad: bfloat16 [2, 2048, 8192], P('dp', 'ctx', 'head'), may hold values from -6 to 6
Outputs:
- mixed_out: bfloat16 [2, 2048, 8192], P('dp', 'ctx', 'head')
- value_grad: bfloat16 [2, 2048, 8192], P('dp', 'ctx', 'head')
- state_grad: bfloat16 [2, 2048, 256], P('dp', 'ctx')
- step_grad: float32 [2, 128, 2048], P('dp', 'head', 'ctx')
- conv_value_grad: float32 [4, 8192], P(None, 'head')
- conv_state_grad: float32 [4, 256], replicated
- head_grads: float32 [3, 128], P(None, 'head')
Inputs may be any that keep to these rules, and one draw needn't show every extreme that they name: `doc_lengths`: each row sums to 2048; its longest document has 1024 tokens.
All inputs are finite; a program needn't handle non-finite values.
Results may differ from a plain program's by a relative error of at most 0.001.
Values may be sent and summed in bfloat16 or wider, within the bound.
A program may use at most 128 MiB of HBM per device.

v0:
```python
from functools import partial

import jax
import jax.numpy as jnp
from jax import lax
from jax.sharding import PartitionSpec as P

HEAD_DIM = 64
STATE = 128
KERNEL = 4
BLOCK = 256


precise = lax.Precision.HIGHEST


def shifted(value, axis, steps):
    count = lax.axis_size(axis)
    leading, last = (max(0, -steps), min(count, count - steps))
    return lax.ppermute(value, axis, [(source, source + steps) for source in range(leading, last)])


def token_starts(lengths, positions):
    doc_ends = jnp.cumsum(lengths)
    passed = doc_ends[None, :] <= positions[:, None]
    return jnp.sum(jnp.where(passed, lengths[None, :], 0), axis=1)


def causal_conv(series, weights, positions, starts, rim_rows):
    padded = jnp.concatenate([rim_rows, series], axis=0)
    length = series.shape[0]
    summed = jnp.zeros(series.shape, jnp.float32)
    for offset in range(KERNEL):
        source = positions - (KERNEL - 1) + offset
        usable = (source >= starts).astype(jnp.float32)
        summed = (
            summed + weights[offset][None, :] * padded[offset : offset + length] * usable[:, None]
        )
    return jax.nn.silu(summed)


def block_pass(carried_in, values, write_rows, read_rows, log_decay, step_sizes, positions, starts):
    block_start = positions[0]
    cumulative = jnp.cumsum(log_decay, axis=1)
    scores = jnp.dot(read_rows, write_rows.T, precision=precise)
    allowed = (positions[None, :] <= positions[:, None]) & (positions[None, :] >= starts[:, None])
    log_gaps = jnp.where(allowed[None], cumulative[:, :, None] - cumulative[:, None, :], 0.0)
    weights = (
        jnp.where(allowed[None], jnp.exp(log_gaps), 0.0) * scores[None] * step_sizes[:, None, :]
    )
    within = jnp.einsum("hts,hsp->htp", weights, values, precision=precise)
    entering = jnp.exp(cumulative) * (starts < block_start).astype(jnp.float32)[None, :]
    carried = jnp.einsum("tn,hpn->htp", read_rows, carried_in, precision=precise)
    within = within + entering[:, :, None] * carried
    tail_keep = (positions >= starts[-1]).astype(jnp.float32)
    tail_weight = jnp.exp(cumulative[:, -1:] - cumulative) * tail_keep[None, :] * step_sizes
    fresh_state = jnp.einsum(
        "hsp,sn->hpn", tail_weight[:, :, None] * values, write_rows, precision=precise
    )
    keep_last = jnp.exp(cumulative[:, -1]) * (starts[-1] < block_start).astype(jnp.float32)
    return (keep_last[:, None, None] * carried_in + fresh_state, within)


def run_blocks(by_head, write_rows, read_rows, log_decay, step_sizes, positions, starts):
    head_count, seq_len, head_width = by_head.shape
    blocks = seq_len // BLOCK

    def one_block(carried_in, block_index):
        block_low = block_index * BLOCK
        return block_pass(
            carried_in,
            lax.dynamic_slice_in_dim(by_head, block_low, BLOCK, 1),
            lax.dynamic_slice_in_dim(write_rows, block_low, BLOCK, 0),
            lax.dynamic_slice_in_dim(read_rows, block_low, BLOCK, 0),
            lax.dynamic_slice_in_dim(log_decay, block_low, BLOCK, 1),
            lax.dynamic_slice_in_dim(step_sizes, block_low, BLOCK, 1),
            lax.dynamic_slice_in_dim(positions, block_low, BLOCK, 0),
            lax.dynamic_slice_in_dim(starts, block_low, BLOCK, 0),
        )

    initial = jnp.zeros((head_count, head_width, write_rows.shape[1]), jnp.float32)
    closing, outputs = lax.scan(
        jax.checkpoint(one_block), initial, jnp.arange(blocks, dtype=jnp.int32)
    )
    return (outputs.transpose(1, 0, 2, 3).reshape(head_count, seq_len, head_width), closing)


def device_forward(
    value_in,
    incoming_state,
    value_rim,
    state_rim,
    step_in,
    conv_value,
    conv_state,
    step_bias,
    decay_log,
    skip_gain,
    positions,
    starts,
    dev_start,
):
    values = causal_conv(value_in, conv_value, positions, starts, value_rim)
    projected = causal_conv(incoming_state, conv_state, positions, starts, state_rim)
    write_rows = projected[:, :STATE]
    read_rows = projected[:, STATE:]
    step_sizes = jax.nn.softplus(step_in + step_bias[:, None])
    log_decay = -jnp.exp(decay_log)[:, None] * step_sizes
    head_count, seq_len = step_sizes.shape
    by_head = values.reshape(seq_len, head_count, HEAD_DIM).transpose(1, 0, 2)
    mixed_heads, fresh_state = run_blocks(
        by_head, write_rows, read_rows, log_decay, step_sizes, positions, starts
    )
    mixed_heads = mixed_heads + skip_gain[:, None, None] * by_head
    running = jnp.cumsum(log_decay, axis=1)
    carry_weight = jnp.exp(running) * (starts < dev_start).astype(jnp.float32)[None, :]
    local_out = mixed_heads.transpose(1, 0, 2).reshape(seq_len, head_count * HEAD_DIM)
    return (local_out, fresh_state, carry_weight[:, -1], carry_weight, read_rows)


def on_device(
    value_input,
    state_proj,
    step_raw,
    doc_lengths,
    conv_value,
    conv_state,
    step_bias,
    decay_log,
    skip_gain,
    out_grad,
):
    seq_len = value_input.shape[1]
    ctx_place = lax.axis_index("ctx")
    context_count = lax.axis_size("ctx")
    dev_start = ctx_place * seq_len
    positions = dev_start + jnp.arange(seq_len, dtype=jnp.int32)
    starts = token_starts(doc_lengths[0], positions)
    tail_rows = seq_len - KERNEL + 1
    value_rim, state_rim = shifted(
        (value_input[0, tail_rows:], state_proj[0, tail_rows:]), "ctx", 1
    )
    forward = partial(device_forward, positions=positions, starts=starts, dev_start=dev_start)
    outputs, pullback = jax.vjp(
        forward,
        value_input[0].astype(jnp.float32),
        state_proj[0].astype(jnp.float32),
        value_rim.astype(jnp.float32),
        state_rim.astype(jnp.float32),
        step_raw[0],
        conv_value,
        conv_state,
        step_bias,
        decay_log,
        skip_gain,
    )
    local_out, fresh_state, keep_decay, carry_weight, read_rows = outputs
    head_count = carry_weight.shape[0]
    grad_flat = out_grad[0].astype(jnp.float32)
    grad_heads = grad_flat.reshape(seq_len, head_count, HEAD_DIM).transpose(1, 0, 2)
    weighted = grad_heads * carry_weight[:, :, None]
    back_local = jnp.einsum("htp,tn->hpn", weighted, read_rows, precision=precise)

    def pass_both(step_turn, pair):
        incoming, outgoing = pair
        ahead = shifted(keep_decay[:, None, None] * incoming + fresh_state, "ctx", 1)
        behind = shifted(keep_decay[:, None, None] * outgoing + back_local, "ctx", -1)
        return (ahead, behind)

    entering, leaving = lax.fori_loop(
        0, context_count - 1, pass_both, (jnp.zeros_like(fresh_state), jnp.zeros_like(back_local))
    )
    carried = jnp.einsum("tn,hpn->htp", read_rows, entering, precision=precise)
    carried_flat = (
        (carry_weight[:, :, None] * carried)
        .transpose(1, 0, 2)
        .reshape(seq_len, head_count * HEAD_DIM)
    )
    mixed_out = (local_out + carried_flat).astype(jnp.bfloat16)[None]
    keep_grad = jnp.sum(leaving * entering, axis=(1, 2))
    weight_grad = jnp.sum(grad_heads * carried, axis=2)
    read_grad = jnp.einsum("htp,hpn->tn", weighted, entering, precision=precise)
    gradients = pullback((grad_flat, leaving, keep_grad, weight_grad, read_grad))
    rim_value, rim_state = shifted((gradients[2], gradients[3]), "ctx", -1)
    value_total = gradients[0].at[tail_rows:].add(rim_value)
    state_partial = gradients[1].at[tail_rows:].add(rim_state)
    state_grad = lax.psum(state_partial, "head").astype(jnp.bfloat16)
    conv_value_grad, head_grads = lax.psum(
        (gradients[5], jnp.stack([gradients[7], gradients[8], gradients[9]])), ("dp", "ctx")
    )
    conv_state_grad = lax.psum(gradients[6], ("dp", "ctx", "head"))
    return (
        mixed_out,
        value_total.astype(jnp.bfloat16)[None],
        state_grad[None],
        gradients[4][None],
        conv_value_grad,
        conv_state_grad,
        head_grads,
    )


def solution(mesh):
    return jax.shard_map(
        on_device,
        mesh=mesh,
        in_specs=(
            P("dp", "ctx", "head"),
            P("dp", "ctx", None),
            P("dp", "head", "ctx"),
            P("dp", None),
            P(None, "head"),
            P(),
            P("head"),
            P("head"),
            P("head"),
            P("dp", "ctx", "head"),
        ),
        out_specs=(
            P("dp", "ctx", "head"),
            P("dp", "ctx", "head"),
            P("dp", "ctx", None),
            P("dp", "head", "ctx"),
            P(None, "head"),
            P(),
            P(None, "head"),
        ),
        check_vma=False,
    )
```

profile of v0, /device:TPU:0, one launch (start us, length us, event | category | flops | bytes accessed | tf_op | source)
XLA Modules:
  0.0 656.6 jit_solution(11228863053123343641)
XLA Ops:
  38.9 6.2 fusion.117
  50.5 47.0 %while.58 = (s32[]{:T(128)}, f32[32,64,128]{2,1,0:T(8,128)S(1)}, f32[2,32,256,64]{2,3,1,0:T(8,128)}, f32[2,32,64,128]{3,2,1,0:T(8,128)}, s32[2]{0:T(128)S(1)}, /...) while((s32[]{:T(128)}, f32[32,64,128]{2,1,0:T(8,128)S(1)}, ...), condition=%wide.region_5.6_spmd.clone, body=%wide.region_2.5_spmd.clone.sunk | while | flops 3336545280 | bytes 84559048 | solution.py:82
  57.3 12.2 %fusion.250 = f32[32,256,64]{1,2,0:T(8,128)S(1)} fusion(f32[32,256]{1,0:T(8,128)S(1)} %get-tuple-element.1206, f32[256,256]{1,0:T(8,128)S(1)} %fusion.249, f32[32,256]{1,0:T(8,128)S(1)} %copy_bitcast_fusion.12, pred[256,256]{1,0:T(8,128)(4,1)S(1)} %compare_and_fusion.5, f32[32,512,64]{1,2,0:T(8,128)} %get-tuple-element.1251, s32[]{:T(128)S(6)} %select_n.201), kind=kOutput, calls=%fused_computation.100.clone.1 | convolution fusion | flops 1621098496 | bytes 4620292 | tf_op jit(solution)/shard_map/jvp()/while/body/eval_jaxpr/hts,hsp->htp/dot_general | solution.py:51
  80.7 12.2 %fusion.250 = f32[32,256,64]{1,2,0:T(8,128)S(1)} fusion(f32[32,256]{1,0:T(8,128)S(1)} %get-tuple-element.1206, f32[256,256]{1,0:T(8,128)S(1)} %fusion.249, f32[32,256]{1,0:T(8,128)S(1)} %copy_bitcast_fusion.12, pred[256,256]{1,0:T(8,128)(4,1)S(1)} %compare_and_fusion.5, f32[32,512,64]{1,2,0:T(8,128)} %get-tuple-element.1251, s32[]{:T(128)S(6)} %select_n.201), kind=kOutput, calls=%fused_computation.100.clone.1 | convolution fusion | flops 1621098496 | bytes 4620292 | tf_op jit(solution)/shard_map/jvp()/while/body/eval_jaxpr/hts,hsp->htp/dot_general | solution.py:51
  98.4 150.3 %while.56 = (s32[]{:T(128)}, f32[32,64,128]{2,1,0:T(8,128)S(1)}, f32[32,64,128]{2,1,0:T(8,128)S(1)}, f32[32,1]{0,1:T(1,128)S(1)}, f32[32,64,128]{2,1,0:T(8,128)S(1)}, /*index=5*/f32[32,64,128]{2,1,0:T(8,128)}, s32[]{:T(128)}) while((s32[]{:T(128)}, f32[32,64,128]{2,1,0:T(8,128)S(1)}, f32[32,64,128]{2,1,0:T(8,128)S(1)}, ...), condition=%wide.region_9.10_spmd, body=%wide.region_8.9_spmd.sunk | while | flops 1048578 | bytes 14680349 | solution.py:170
  106.1 20.8 %collective-permute-done = f32[32,64,128]{2,1,0:T(8,128)S(1)} collective-permute-done((f32[32,64,128]{2,1,0:T(8,128)}, f32[32,64,128]{2,1,0:T(8,128)S(1)}, u32[]{:S(2)}, u32[]{:S(2)}) %collective-permute-start) | collective-permute-done | bytes 1048608 | tf_op jit(solution)/shard_map/while/body/eval_jaxpr/ppermute | solution.py:20
  126.9 23.1 %collective-permute-done.1 = f32[32,64,128]{2,1,0:T(8,128)S(1)} collective-permute-done((f32[32,64,128]{2,1,0:T(8,128)}, f32[32,64,128]{2,1,0:T(8,128)S(1)}, u32[]{:S(2)}, u32[]{:S(2)}) %collective-permute-start.1) | collective-permute-done | bytes 1048608 | tf_op jit(solution)/shard_map/while/body/eval_jaxpr/ppermute | solution.py:20
  156.4 20.5 %collective-permute-done = f32[32,64,128]{2,1,0:T(8,128)S(1)} collective-permute-done((f32[32,64,128]{2,1,0:T(8,128)}, f32[32,64,128]{2,1,0:T(8,128)S(1)}, u32[]{:S(2)}, u32[]{:S(2)}) %collective-permute-start) | collective-permute-done | bytes 1048608 | tf_op jit(solution)/shard_map/while/body/eval_jaxpr/ppermute | solution.py:20
  176.9 23.1 %collective-permute-done.1 = f32[32,64,128]{2,1,0:T(8,128)S(1)} collective-permute-done((f32[32,64,128]{2,1,0:T(8,128)}, f32[32,64,128]{2,1,0:T(8,128)S(1)}, u32[]{:S(2)}, u32[]{:S(2)}) %collective-permute-start.1) | collective-permute-done | bytes 1048608 | tf_op jit(solution)/shard_map/while/body/eval_jaxpr/ppermute | solution.py:20
  205.8 19.8 %collective-permute-done = f32[32,64,128]{2,1,0:T(8,128)S(1)} collective-permute-done((f32[32,64,128]{2,1,0:T(8,128)}, f32[32,64,128]{2,1,0:T(8,128)S(1)}, u32[]{:S(2)}, u32[]{:S(2)}) %collective-permute-start) | collective-permute-done | bytes 1048608 | tf_op jit(solution)/shard_map/while/body/eval_jaxpr/ppermute | solution.py:20
  225.6 23.1 %collective-permute-done.1 = f32[32,64,128]{2,1,0:T(8,128)S(1)} collective-permute-done((f32[32,64,128]{2,1,0:T(8,128)}, f32[32,64,128]{2,1,0:T(8,128)S(1)}, u32[]{:S(2)}, u32[]{:S(2)}) %collective-permute-start.1) | collective-permute-done | bytes 1048608 | tf_op jit(solution)/shard_map/while/body/eval_jaxpr/ppermute | solution.py:20
  255.3 216.8 %while.57 = (s32[]{:T(128)}, f32[32,512,64]{1,2,0:T(8,128)}, f32[512,128]{1,0:T(8,128)}, f32[512,128]{1,0:T(8,128)}, f32[32,512]{1,0:T(8,128)}, /*index=5*/f32[3...) while((s32[]{:T(128)}, f32[32,512,64]{1,2,0:T(8,128)}, ...), condition=%wide.region_23.24_spmd.clone, body=%wide.region_10.23_spmd.clone.sunk | while | flops 7600506368 | bytes 93365344 | solution.py:82
  309.0 16.1 %fusion.231 = (f32[32,256]{1,0:T(8,128)}, f32[32,256]{1,0:T(8,128)}, f32[32,256]{1,0:T(8,128)}, f32[256,256]{1,0:T(8,128)}) fusion(f32[32,256]{1,0:T(8,128)} %copy.266, f32[256,256]{1,0:T(8,128)} %fusion.230, f32[32,256]{1,0:T(8,128)} %copy_bitcast_fusion.10, pred[256,256]{1,0:T(8,128)(4,1)} %compare_and_fusion.4, ...), kind=kOutput, calls=%fused_computation.12.clone.1 | convolution fusion | flops 1641979904 | bytes 4980740 | tf_op jit(solution)/shard_map/transpose(jvp())/while/body/eval_jaxpr/checkpoint/hts,hsp->htp/dot_general | solution.py:51
  359.4 7.8 %fusion.233 = f32[32,512,64]{1,2,0:T(8,128)S(1)} fusion(f32[32,512,64]{1,2,0:T(8,128)S(1)} %copy-done.14, s32[]{:T(128)S(6)} %select_n.198, f32[32,64,256]{2,1,0:T(8,128)S(1)} %copy-done.10, f32[32,256,64]{1,2,0:T(8,128)S(1)} %dynamic-slice_bitcast_fusion.12, f32[32,256]{1,0:T(8,128)S(1)} %copy-done.49, f32[256,256]{1,0:T(8,128)S(1)} %copy-done.27, ...), kind=kOutput, calls=%fused_computation.29.clone.1 | convolution fusion | flops 1622671360 | bytes 8847364 | tf_op jit(solution)/shard_map/transpose(jvp())/while/body/eval_jaxpr/checkpoint/hts,hsp->htp/dot_general | solution.py:51
  403.5 16.1 %fusion.231 = (f32[32,256]{1,0:T(8,128)}, f32[32,256]{1,0:T(8,128)}, f32[32,256]{1,0:T(8,128)}, f32[256,256]{1,0:T(8,128)}) fusion(f32[32,256]{1,0:T(8,128)} %copy.266, f32[256,256]{1,0:T(8,128)} %fusion.230, f32[32,256]{1,0:T(8,128)} %copy_bitcast_fusion.10, pred[256,256]{1,0:T(8,128)(4,1)} %compare_and_fusion.4, ...), kind=kOutput, calls=%fused_computation.12.clone.1 | convolution fusion | flops 1641979904 | bytes 4980740 | tf_op jit(solution)/shard_map/transpose(jvp())/while/body/eval_jaxpr/checkpoint/hts,hsp->htp/dot_general | solution.py:51
  453.9 7.8 %fusion.233 = f32[32,512,64]{1,2,0:T(8,128)S(1)} fusion(f32[32,512,64]{1,2,0:T(8,128)S(1)} %copy-done.14, s32[]{:T(128)S(6)} %select_n.198, f32[32,64,256]{2,1,0:T(8,128)S(1)} %copy-done.10, f32[32,256,64]{1,2,0:T(8,128)S(1)} %dynamic-slice_bitcast_fusion.12, f32[32,256]{1,0:T(8,128)S(1)} %copy-done.49, f32[256,256]{1,0:T(8,128)S(1)} %copy-done.27, ...), kind=kOutput, calls=%fused_computation.29.clone.1 | convolution fusion | flops 1622671360 | bytes 8847364 | tf_op jit(solution)/shard_map/transpose(jvp())/while/body/eval_jaxpr/checkpoint/hts,hsp->htp/dot_general | solution.py:51
  472.3 9.4 %fusion.127 = f32[512,128]{1,0:T(8,128)S(1)} fusion(f32[512,128]{1,0:T(8,128)} %get-tuple-element.553, f32[32,64,128]{2,1,0:T(8,128)} %copy-done.4, f32[32,512,64]{1,2,0:T(8,128)} %bitcast.345, f32[32,512]{1,0:T(8,128)} %copy-done.50), kind=kOutput, calls=%fused_computation.189 | convolution fusion | flops 1611726848 | bytes 5832704 | tf_op jit(solution)/shard_map/htp,hpn->tn/dot_general | solution.py:182
  494.1 6.2 multiply_reduce_fusion.3
  505.9 11.1 %multiply_reduce_fusion.6 = (f32[2048]{0:T(1024)}, f32[2048]{0:T(1024)}, f32[2048]{0:T(1024)}, f32[2048]{0:T(1024)}, f32[512,2048]{1,0:T(8,128)S(1)}) fusion(f32[512,2048]{1,0:T(8,128)} %bitcast_convert_fusion, f32[3,2048]{1,0:T(4,128)S(1)} %copy-done.53, f32[512]{0:T(512)S(1)} %copy-done.62, f32[512]{0:T(512)S(1)} %copy-done.64, f32[512]{0:T(512)S(1)} %copy-done.58, ...), kind=kLoop, calls=%fused_computation.170 | loop fusion | flops 26206208 | bytes 18939904 | tf_op jit(solution)/shard_map/transpose(jvp())/reduce_sum | solution.py:37
  524.5 5.6 pad_add_fusion
  537.1 5.7 reduce-window.89
  548.7 30.4 %all-reduce.21 = (f32[4,2048]{1,0:T(4,128)}, f32[3,32]{1,0:T(4,128)}) all-reduce(f32[4,2048]{1,0:T(4,128)S(1)} %pad_add_fusion.3, f32[3,32]{1,0:T(4,128)S(1)} %pad_maximum_fusion.2), channel_id=1, replica_groups=mesh['dp'=2,'ctx'=4,'head'=4] {'dp','ctx'}, use_global_device_ids=true, to_apply=%region_33.34 | all-reduce | flops 8288 | bytes 66304 | tf_op jit(solution)/shard_map/psum | solution.py:188
  582.8 39.9 %psum.30 = f32[4,256]{1,0:T(4,128)} all-reduce(f32[4,256]{1,0:T(4,128)S(1)} %pad_add_fusion.5), channel_id=1, replica_groups=mesh['dp'=2,'ctx'=4,'head'=4] {'dp','ctx','head'}, use_global_device_ids=true, to_apply=%region_38.39 | all-reduce | flops 1024 | bytes 8192 | tf_op jit(solution)/shard_map/psum | solution.py:191
  624.7 29.3 %all-reduce.23 = bf16[512,256]{1,0:T(8,128)(2,1)} all-reduce(f32[512,256]{1,0:T(8,128)} %scatter-add.9), channel_id=1, replica_groups=mesh['dp'=2,'ctx'=4,'head'=4] {'head'}, use_global_device_ids=true, to_apply=%region_24.25 | all-reduce | flops 131072 | bytes 786432 | tf_op jit(solution)/shard_map/psum | solution.py:187
  (447 shorter events, 272.2 us)
Async XLA Ops:
  0.6 22.1 %copy-start.77 = (f32[4,2048]{1,0:T(4,128)S(1)}, f32[4,2048]{1,0:T(4,128)}, u32[]{:S(2)}) copy-start(f32[4,2048]{1,0:T(4,128)} %param.24) | copy-start | bytes 98308
  0.6 22.2 %copy-start.88 = (f32[4,256]{1,0:T(4,128)S(1)}, f32[4,256]{1,0:T(4,128)}, u32[]{:S(2)}) copy-start(f32[4,256]{1,0:T(4,128)} %param.25) | copy-start | bytes 12292
  1.4 31.6 %collective-permute-start.3 = (bf16[3,256]{1,0:T(4,128)(2,1)S(1)}, bf16[3,256]{1,0:T(4,128)(2,1)S(1)}, u32[]{:S(2)}, u32[]{:S(2)}) collective-permute-start(bf16[3,256]{1,0:T(4,128)(2,1)S(1)} %slice_bitcast_fusion.2), channel_id=1, source_target_pairs={{0,4},{4,8},{8,12},{1,5},{5,9},{9,13},{2,6},{6,10},{10,14},{3,7},{... | collective-permute-start | bytes 4616 | tf_op jit(solution)/shard_map/ppermute | solution.py:20
  7.0 31.8 %collective-permute-start.2 = (bf16[3,2048]{1,0:T(4,128)(2,1)S(1)}, bf16[3,2048]{1,0:T(4,128)(2,1)S(1)}, u32[]{:S(2)}, u32[]{:S(2)}) collective-permute-start(bf16[3,2048]{1,0:T(4,128)(2,1)S(1)} %slice_bitcast_fusion.1), channel_id=1, source_target_pairs={{0,4},{4,8},{8,12},{1,5},{5,9},{9,13},{2,6},{6,10},{10,14},{3,7},{... | collective-permute-start | bytes 36872 | tf_op jit(solution)/shard_map/ppermute | solution.py:20
  12.6 26.1 %copy-start.57 = (f32[512]{0:T(512)}, f32[512]{0:T(512)S(1)}, u32[]{:S(2)}) copy-start(f32[512]{0:T(512)S(1)} %get-tuple-element.916) | copy-start | bytes 6148
  12.6 26.1 %copy-start.59 = (f32[512]{0:T(512)}, f32[512]{0:T(512)S(1)}, u32[]{:S(2)}) copy-start(f32[512]{0:T(512)S(1)} %get-tuple-element.918) | copy-start | bytes 6148
  12.7 26.1 %copy-start.61 = (f32[512]{0:T(512)}, f32[512]{0:T(512)S(1)}, u32[]{:S(2)}) copy-start(f32[512]{0:T(512)S(1)} %get-tuple-element.919) | copy-start | bytes 6148
  12.7 26.1 %copy-start.63 = (f32[512]{0:T(512)}, f32[512]{0:T(512)S(1)}, u32[]{:S(2)}) copy-start(f32[512]{0:T(512)S(1)} %get-tuple-element.920) | copy-start | bytes 6148
  15.8 18.4 %copy-start.50 = (f32[32,512]{1,0:T(8,128)}, f32[32,512]{1,0:T(8,128)S(1)}, u32[]{:S(2)}) copy-start(f32[32,512]{1,0:T(8,128)S(1)} %bitcast_multiply_fusion.8) | copy-start | bytes 196612
  22.8 16.0 %copy-start.65 = (f32[1,2048]{1,0:T(1,128)}, f32[1,2048]{1,0:T(1,128)S(1)}, u32[]{:S(2)}) copy-start(f32[1,2048]{1,0:T(1,128)S(1)} %get-tuple-element.908) | copy-start | bytes 24580
  22.8 16.0 %copy-start.67 = (f32[1,2048]{1,0:T(1,128)}, f32[1,2048]{1,0:T(1,128)S(1)}, u32[]{:S(2)}) copy-start(f32[1,2048]{1,0:T(1,128)S(1)} %get-tuple-element.909) | copy-start | bytes 24580
  101.3 25.5 %collective-permute-start = (f32[32,64,128]{2,1,0:T(8,128)}, f32[32,64,128]{2,1,0:T(8,128)S(1)}, u32[]{:S(2)}, u32[]{:S(2)}) collective-permute-start(f32[32,64,128]{2,1,0:T(8,128)} %get-tuple-element.1143), channel_id=1, source_target_pairs={{0,4},{4,8},{8,12},{1,5},{5,9},{9,13},{2,6},{6,10},{10,14},{3,7},{... | collective-permute-start | bytes 3145736 | tf_op jit(solution)/shard_map/while/body/eval_jaxpr/ppermute | solution.py:20
  104.8 45.2 %collective-permute-start.1 = (f32[32,64,128]{2,1,0:T(8,128)}, f32[32,64,128]{2,1,0:T(8,128)S(1)}, u32[]{:S(2)}, u32[]{:S(2)}) collective-permute-start(f32[32,64,128]{2,1,0:T(8,128)} %get-tuple-element.1144), channel_id=1, source_target_pairs={{4,0},{8,4},{12,8},{5,1},{9,5},{13,9},{6,2},{10,6},{14,10},{7,3},{... | collective-permute-start | bytes 3145736 | tf_op jit(solution)/shard_map/while/body/eval_jaxpr/ppermute | solution.py:20
  152.9 24.0 %collective-permute-start = (f32[32,64,128]{2,1,0:T(8,128)}, f32[32,64,128]{2,1,0:T(8,128)S(1)}, u32[]{:S(2)}, u32[]{:S(2)}) collective-permute-start(f32[32,64,128]{2,1,0:T(8,128)} %get-tuple-element.1143), channel_id=1, source_target_pairs={{0,4},{4,8},{8,12},{1,5},{5,9},{9,13},{2,6},{6,10},{10,14},{3,7},{... | collective-permute-start | bytes 3145736 | tf_op jit(solution)/shard_map/while/body/eval_jaxpr/ppermute | solution.py:20
  155.1 44.9 %collective-permute-start.1 = (f32[32,64,128]{2,1,0:T(8,128)}, f32[32,64,128]{2,1,0:T(8,128)S(1)}, u32[]{:S(2)}, u32[]{:S(2)}) collective-permute-start(f32[32,64,128]{2,1,0:T(8,128)} %get-tuple-element.1144), channel_id=1, source_target_pairs={{4,0},{8,4},{12,8},{5,1},{9,5},{13,9},{6,2},{10,6},{14,10},{7,3},{... | collective-permute-start | bytes 3145736 | tf_op jit(solution)/shard_map/while/body/eval_jaxpr/ppermute | solution.py:20
  202.9 22.8 %collective-permute-start = (f32[32,64,128]{2,1,0:T(8,128)}, f32[32,64,128]{2,1,0:T(8,128)S(1)}, u32[]{:S(2)}, u32[]{:S(2)}) collective-permute-start(f32[32,64,128]{2,1,0:T(8,128)} %get-tuple-element.1143), channel_id=1, source_target_pairs={{0,4},{4,8},{8,12},{1,5},{5,9},{9,13},{2,6},{6,10},{10,14},{3,7},{... | collective-permute-start | bytes 3145736 | tf_op jit(solution)/shard_map/while/body/eval_jaxpr/ppermute | solution.py:20
  204.5 44.2 %collective-permute-start.1 = (f32[32,64,128]{2,1,0:T(8,128)}, f32[32,64,128]{2,1,0:T(8,128)S(1)}, u32[]{:S(2)}, u32[]{:S(2)}) collective-permute-start(f32[32,64,128]{2,1,0:T(8,128)} %get-tuple-element.1144), channel_id=1, source_target_pairs={{4,0},{8,4},{12,8},{5,1},{9,5},{13,9},{6,2},{10,6},{14,10},{7,3},{... | collective-permute-start | bytes 3145736 | tf_op jit(solution)/shard_map/while/body/eval_jaxpr/ppermute | solution.py:20
  334.9 22.0 %copy-start.78 = (f32[32]{0:T(128)S(1)}, f32[32]{0:T(128)}, u32[]{:S(2)}) copy-start(f32[32]{0:T(128)} %exponential_multiply_fusion.6) | copy-start | bytes 388 | tf_op jit(solution)/shard_map/transpose(jvp())/while
  429.5 22.0 %copy-start.78 = (f32[32]{0:T(128)S(1)}, f32[32]{0:T(128)}, u32[]{:S(2)}) copy-start(f32[32]{0:T(128)} %exponential_multiply_fusion.6) | copy-start | bytes 388 | tf_op jit(solution)/shard_map/transpose(jvp())/while
  530.1 50.8 %copy-start.19 = (bf16[515,2048]{1,0:T(8,128)(2,1)S(1)}, bf16[515,2048]{1,0:T(8,128)(2,1)}, u32[]{:S(2)}) copy-start(bf16[515,2048]{1,0:T(8,128)(2,1)} %pad_add_fusion) | copy-start | bytes 6328324
  530.2 92.4 %collective-permute-start.5 = (f32[3,256]{1,0:T(4,128)}, f32[3,256]{1,0:T(4,128)}, u32[]{:S(2)}, u32[]{:S(2)}) collective-permute-start(f32[3,256]{1,0:T(4,128)} %pad_add_fusion.4), channel_id=1, source_target_pairs={{4,0},{8,4},{12,8},{5,1},{9,5},{13,9},{6,2},{10,6},{14,10},{7,3},{... | collective-permute-start | bytes 9224 | tf_op jit(solution)/shard_map/ppermute | solution.py:20
  531.6 91.0 %copy-start.21 = (f32[512,256]{1,0:T(8,128)S(1)}, f32[512,256]{1,0:T(8,128)}, u32[]{:S(2)}) copy-start(f32[512,256]{1,0:T(8,128)} %copy-done.20) | copy-start | bytes 1572868
  531.6 91.0 %copy-start.23 = (f32[512,256]{1,0:T(8,128)S(1)}, f32[512,256]{1,0:T(8,128)}, u32[]{:S(2)}) copy-start(f32[512,256]{1,0:T(8,128)} %copy-done.22) | copy-start | bytes 1572868
  545.2 108.8 %collective-permute-start.4 = (f32[3,2048]{1,0:T(4,128)S(1)}, f32[3,2048]{1,0:T(4,128)S(1)}, u32[]{:S(2)}, u32[]{:S(2)}) collective-permute-start(f32[3,2048]{1,0:T(4,128)S(1)} %pad_add_fusion.2), channel_id=1, source_target_pairs={{4,0},{8,4},{12,8},{5,1},{9,5},{13,9},{6,2},{10,6},{14,10},{7,3},{... | collective-permute-start | bytes 73736 | tf_op jit(solution)/shard_map/ppermute | solution.py:20
  (99 other events, 770.4 us)
where the time goes:
time: 666 us; the launch traced here: 657 us
  matrix products  151 us (23%)
  waiting for transfers between devices  130 us (20%)
  local copies, waits for them, and re-layouts  109 us (16%)
  other arithmetic  107 us (16%)
  blocking collectives  99.6 us (15%)
  loops' own time  36.3 us (5%)
  starting transfers between devices  22.1 us (3%)
    ppermute x10, waiting for transfers between devices, shifted(): lax.ppermute(value, axis, [(source, source + steps) for source in range(l...  130 us
    dot_general x6, matrix products, block_pass(): within = jnp.einsum('hts,hsp->htp', weights, values, precision=precise)  72.1 us
    psum x1, blocking collectives, on_device(): conv_state_grad = lax.psum(gradients[6], ('dp', 'ctx', 'head'))  39.9 us
    another operation x2, loops' own time, run_blocks(): lax.scan(jax.checkpoint(one_block), initial, jnp.arange(blocks, dtype=jnp...  36.2 us
    psum x1, blocking collectives, on_device(): lax.psum((gradients[5], jnp.stack([gradients[7], gradients[8], gradients[...  30.4 us
    psum x1, blocking collectives, on_device(): state_grad = lax.psum(state_partial, 'head').astype(jnp.bfloat16)  29.3 us
    dot_general x6, matrix products, block_pass(): jnp.einsum('hsp,sn->hpn', tail_weight[:, :, None] * values, write_rows, p...  25.5 us
    dot_general x8, matrix products, block_pass(): jnp.einsum('tn,hpn->htp', read_rows, carried_in, precision=precise)  23.7 us
  transfers between devices with their start and end apart: 10, of which 6 were waited for; matrix products, arithmetic and copies ran while one was open for 8% of the time, Pallas kernels for 0%

commit v1 on v0

v1 whole, which is shorter than its diff:
```python
from functools import partial

import jax
import jax.numpy as jnp
from jax import lax
from jax.experimental import pallas as pl
from jax.experimental.pallas import tpu as pltpu
from jax.sharding import PartitionSpec as P

HEAD_DIM = 64
STATE = 128
KERNEL = 4
SUB = 128
PAIR = 2
LANES = PAIR * HEAD_DIM
LOG2E = 1.4426950408889634

precise = lax.Precision.HIGHEST
f32 = jnp.float32
bf16 = jnp.bfloat16


def shifted(value, axis, steps):
    count = lax.axis_size(axis)
    leading, last = (max(0, -steps), min(count, count - steps))
    return lax.ppermute(value, axis, [(source, source + steps) for source in range(leading, last)])


def token_starts(lengths, positions):
    doc_ends = jnp.cumsum(lengths)
    passed = doc_ends[None, :] <= positions[:, None]
    return jnp.sum(jnp.where(passed, lengths[None, :], 0), axis=1)


def causal_conv(series, weights, usable, rim_rows):
    padded = jnp.concatenate([rim_rows, series], axis=0)
    length = series.shape[0]
    summed = jnp.zeros(series.shape, f32)
    for offset in range(KERNEL):
        summed = summed + weights[offset][None, :] * padded[offset : offset + length] * usable[offset][:, None]
    return jax.nn.silu(summed)


def split(value):
    high = value.astype(bf16)
    return high, (value - high.astype(f32)).astype(bf16)


def mm(a, b):
    return jnp.dot(a, b, preferred_element_type=f32)


def mm_nt(a, b):
    return lax.dot_general(a, b, (((1,), (1,)), ((), ())), preferred_element_type=f32)


def mm3(a, b):
    (ah, al), (bh, bl) = a, b
    return mm(ah, bh) + (mm(al, bh) + mm(ah, bl))


def mm3_nt(a, b):
    (ah, al), (bh, bl) = a, b
    return mm_nt(ah, bh) + (mm_nt(al, bh) + mm_nt(ah, bl))


def first_lanes(rows):
    return lax.broadcasted_iota(jnp.int32, (rows, LANES), 1) < HEAD_DIM


def spread(columns, which):
    left = columns[:, PAIR * which : PAIR * which + 1]
    right = columns[:, PAIR * which + 1 : PAIR * which + 2]
    return jnp.where(first_lanes(columns.shape[0]), left, right)


C_CUM, C_STEP, C_NEAR, C_FAR, C_ENTER, C_LEAVE = range(6)


def sigmoid(value):
    return 1.0 / (1.0 + jnp.exp(-value))


def states_kernel(x, rim, dy, taps, usable, cols, write_t, read_t, pre_out, fresh, back, pad, wt_s, rt_s):
    rows = x.shape[0]

    @pl.when(pl.program_id(0) == 0)
    def _():
        wt_s[0], wt_s[1] = split(write_t[...])
        rt_s[0], rt_s[1] = split(read_t[...])

    pad[0:8] = rim[...]
    pad[8 : 8 + rows] = x[...].astype(f32)
    pre = jnp.zeros((rows, LANES), f32)
    for k in range(KERNEL):
        term = taps[k : k + 1, :] * pad[5 + k : 5 + k + rows]
        if k < KERNEL - 1:
            term = term * usable[:, k * LANES : (k + 1) * LANES]
        pre = pre + term
    pre_out[...] = pre
    columns = cols[0]
    weighted = pre * sigmoid(pre) * (spread(columns, C_STEP) * spread(columns, C_LEAVE))
    fresh[...] = mm3((wt_s[0], wt_s[1]), split(weighted))
    grad = dy[...].astype(f32) * spread(columns, C_ENTER)
    back[...] = mm3((rt_s[0], rt_s[1]), split(grad))


def local_kernel(pre_ref, dy, cols, rows_ref, gram, gram_t, y_out, u_out, dgram, g_s, gt_s):
    rows = dy.shape[0]
    blocks = rows // SUB
    half = rows // 2

    @pl.when(pl.program_id(0) == 0)
    def _():
        dgram[...] = jnp.zeros_like(dgram)
        g_s[0], g_s[1] = split(gram[...])
        gt_s[0], gt_s[1] = split(gram_t[...])

    columns = cols[0]
    lanes = first_lanes(SUB)
    zero = jnp.zeros((SUB, LANES), f32)
    pre = pre_ref[...]
    xs = pre * sigmoid(pre) * spread(columns, C_STEP)
    grad = dy[...].astype(f32)
    for b in range(blocks):
        at = slice(b * SUB, (b + 1) * SUB)
        decays, m, mt = [], [], []
        for j in range(PAIR):
            down = columns[at, j : j + 1]
            across = rows_ref[0, j : j + 1, at]
            gap = down - across
            decay = jnp.exp2(jnp.minimum(gap, 0.0))
            decays.append(decay)
            m.append(gram[at, at] * decay)
            mt.append(gram_t[at, at] * jnp.exp2(jnp.minimum(-gap, 0.0)))
        mh, ml = split(jnp.concatenate(m, axis=1))
        mth, mtl = split(jnp.concatenate(mt, axis=1))
        xb = xs[at]
        high = xb.astype(bf16).astype(f32)
        low = xb - high
        xbh = jnp.concatenate([jnp.where(lanes, high, zero), jnp.where(lanes, zero, high)], axis=0).astype(bf16)
        xbl = jnp.concatenate([jnp.where(lanes, low, zero), jnp.where(lanes, zero, low)], axis=0).astype(bf16)
        gb = grad[at]
        gbd = jnp.concatenate([jnp.where(lanes, gb, zero), jnp.where(lanes, zero, gb)], axis=0).astype(bf16)
        both = mm(mh, jnp.concatenate([xbh, xbl], axis=1))
        y_out[at] = both[:, :LANES] + (both[:, LANES:] + mm(ml, xbh))
        u_out[at] = mm(mth, gbd) + mm(mtl, gbd)
        d = mm_nt(
            jnp.concatenate([gbd, gbd], axis=1),
            jnp.concatenate([high.astype(bf16), low.astype(bf16)], axis=1),
        )
        dgram[at, at] += d[:SUB] * decays[0] + d[SUB:] * decays[1]

    def across_blocks(low, mid, top, which):
        early, late = slice(low, mid), slice(mid, top)
        factor = spread(columns[low:top], which)
        size = mid - low
        fe, fl = factor[:size], factor[size:]
        source = split(fe * xs[early])
        target = split(fl * grad[late])
        y_out[late] += fl * mm3((g_s[0, late, early], g_s[1, late, early]), source)
        u_out[early] += fe * mm3((gt_s[0, early, late], gt_s[1, early, late]), target)
        dgram[late, early] += mm3_nt(target, source)

    for b in range(0, blocks, 2):
        across_blocks(b * SUB, (b + 1) * SUB, (b + 2) * SUB, C_NEAR)
    across_blocks(0, half, rows, C_FAR)


def final_kernel(
    pre_ref, x, rim, dy, cols, usable, taps, skip, projected, entering, leaving, y_in, u_in,
    mixed, vgrad, tail, rim_out, tap_grad, token_sums, skip_sums, dproj,
    pad, dpad, p_s,
):
    rows = dy.shape[0]

    @pl.when(pl.program_id(0) == 0)
    def _():
        dproj[...] = jnp.zeros_like(dproj)
        p_s[0], p_s[1] = split(projected[...])
        dpad[0:8] = jnp.zeros((8, LANES), f32)
        dpad[8 + rows : 16 + rows] = jnp.zeros((8, LANES), f32)

    write = (p_s[0, :, :STATE], p_s[1, :, :STATE])
    read = (p_s[0, :, STATE:], p_s[1, :, STATE:])
    columns = cols[0]
    pre = pre_ref[...]
    gate = sigmoid(pre)
    values = pre * gate
    step = spread(columns, C_STEP)
    grad = dy[...].astype(f32)
    ent = split(entering[...])
    lea = split(leaving[...])
    enter = spread(columns, C_ENTER)
    leave = spread(columns, C_LEAVE)
    y = y_in[...] + enter * mm3(read, ent)
    u = u_in[...] + leave * mm3(write, lea)
    dproj[:, STATE:] += mm3_nt(split(enter * grad), ent)
    dproj[:, :STATE] += mm3_nt(split(leave * step * values), lea)
    gain = skip[0:1, :]
    mixed[...] = (y + gain * values).astype(bf16)
    dvalues = step * u + gain * grad
    skip_sums[0] = jnp.broadcast_to(jnp.sum(grad * values, axis=0, keepdims=True), (8, LANES))
    lane = lax.broadcasted_iota(jnp.int32, (8, LANES), 1) // HEAD_DIM
    row = lax.broadcasted_iota(jnp.int32, (8, LANES), 0)
    chosen = jnp.where(row == lane, 1.0, 0.0).astype(bf16)
    chosen = jnp.concatenate([chosen, chosen], axis=1)
    first = mm_nt(chosen, jnp.concatenate(split(grad * y), axis=1))
    second = mm_nt(chosen, jnp.concatenate(split(values * u), axis=1))
    token_sums[0, 0:2] = first[0:2]
    token_sums[0, 2:4] = second[0:2]
    dpre = dvalues * (gate * (1.0 + pre * (1.0 - gate)))

    pad[0:8] = rim[...]
    pad[8 : 8 + rows] = x[...].astype(f32)
    total = jnp.zeros((rows + 8, LANES), f32)
    for k in range(KERNEL):
        part = dpre
        if k < KERNEL - 1:
            part = part * usable[:, k * LANES : (k + 1) * LANES]
        tap_grad[k : k + 1, :] = jnp.sum(part * pad[5 + k : 5 + k + rows], axis=0, keepdims=True)
        dpad[8 : 8 + rows] = part
        total = total + taps[k : k + 1, :] * dpad[3 - k + 0 : 3 - k + rows + 8]
    rim_out[...] = total[0:8]
    vgrad[...] = total[8:].astype(bf16)
    tail[...] = total[rows:]


def on_device(
    value_input,
    state_proj,
    step_raw,
    doc_lengths,
    conv_value,
    conv_state,
    step_bias,
    decay_log,
    skip_gain,
    out_grad,
    interpret=False,
):
    rows, channels = value_input.shape[1:]
    heads = step_raw.shape[1]
    pairs = heads // PAIR
    blocks = rows // SUB
    half = rows // 2
    rim = KERNEL - 1
    ctx_place = lax.axis_index("ctx")
    context_count = lax.axis_size("ctx")
    whole = rows * context_count
    reach = min(context_count - 1, (whole // 2 - 2) // rows + 1)
    dev_start = ctx_place * rows
    positions = dev_start + jnp.arange(rows, dtype=jnp.int32)
    starts = token_starts(doc_lengths[0], positions)
    x = value_input[0]
    dy = out_grad[0]
    tail_rows = rows - rim
    rims = shifted(jnp.concatenate([x[tail_rows:], state_proj[0, tail_rows:]], axis=1), "ctx", 1)
    value_rim = jnp.concatenate([jnp.zeros((8 - rim, channels), f32), rims[:, :channels].astype(f32)], axis=0)
    state_rim = rims[:, channels:].astype(f32)

    usable = [(positions - rim + k >= starts).astype(f32) for k in range(KERNEL)]
    usable_wide = jnp.concatenate(
        [jnp.broadcast_to(usable[k][:, None], (rows, LANES)) for k in range(rim)], axis=1
    )
    projected, state_pullback = jax.vjp(
        lambda series, weights, rim_rows: causal_conv(series, weights, usable, rim_rows),
        state_proj[0].astype(f32), conv_state, state_rim,
    )
    write_rows, read_rows = projected[:, :STATE], projected[:, STATE:]
    allowed = (positions[None, :] <= positions[:, None]) & (positions[None, :] >= starts[:, None])
    gram = jnp.where(allowed, jnp.dot(read_rows, write_rows.T, precision=precise), 0.0)
    gram_t = jnp.where(allowed.T, jnp.dot(write_rows, read_rows.T, precision=precise), 0.0)

    logits = step_raw[0] + step_bias[:, None]
    step = jax.nn.softplus(logits)
    rate = jnp.exp(decay_log)[:, None]
    log_decay = -rate * step
    index = jnp.arange(SUB)
    upper = (index[:, None] <= index[None, :]).astype(f32)
    cum = jnp.einsum("hbs,st->hbt", log_decay.reshape(heads, blocks, SUB), upper, precision=precise)
    totals = cum[:, :, -1]

    def flat(value):
        return value.reshape(heads, rows)

    def before(first, block):
        return sum((totals[:, i] for i in range(first, block)), jnp.zeros((heads,), f32))

    near, far, enter, leave = [], [], [], []
    for b in range(blocks):
        inner = cum[:, b]
        rest = totals[:, b : b + 1] - inner
        near.append(inner if b % 2 else rest)
        if b >= blocks // 2:
            far.append(inner + before(blocks // 2, b)[:, None])
        else:
            far.append(rest + before(b + 1, blocks // 2)[:, None])
        enter.append(inner + before(0, b)[:, None])
        leave.append(rest + before(b + 1, blocks)[:, None])
    near, far, enter, leave = (jnp.exp(jnp.concatenate(v, axis=1)) for v in (near, far, enter, leave))
    enter = enter * (starts < dev_start).astype(f32)[None]
    leave = leave * (positions >= starts[-1]).astype(f32)[None]
    keep = jnp.exp(before(0, blocks)) * (starts[-1] < dev_start).astype(f32)
    cum2 = flat(cum) * LOG2E
    cols = jnp.stack([cum2, step, near, far, enter, leave])
    cols = cols.reshape(6, pairs, PAIR, rows).transpose(1, 3, 0, 2).reshape(pairs, rows, 6 * PAIR)
    row_form = cum2.reshape(pairs, PAIR, rows)

    col_spec = pl.BlockSpec((rows, LANES), lambda g: (0, g))
    cols_spec = pl.BlockSpec((1, rows, 6 * PAIR), lambda g: (g, 0, 0))
    eight_spec = pl.BlockSpec((8, LANES), lambda g: (0, g))
    taps_spec = pl.BlockSpec((KERNEL, LANES), lambda g: (0, g))
    state_spec = pl.BlockSpec((STATE, LANES), lambda g: (0, g))

    def fixed(*shape):
        return pl.BlockSpec(shape, lambda g: (0,) * len(shape))

    def like(*shape, dtype=f32):
        return jax.ShapeDtypeStruct(shape, dtype)

    params = pltpu.CompilerParams(
        dimension_semantics=("arbitrary",), vmem_limit_bytes=48 * 1024 * 1024
    )
    pre, fresh, back = pl.pallas_call(
        states_kernel,
        grid=(pairs,),
        in_specs=[col_spec, eight_spec, col_spec, taps_spec, fixed(rows, rim * LANES), cols_spec,
                  fixed(STATE, rows), fixed(STATE, rows)],
        out_specs=[col_spec, state_spec, state_spec],
        out_shape=[like(rows, channels), like(STATE, channels), like(STATE, channels)],
        scratch_shapes=[pltpu.VMEM((rows + 8, LANES), f32), pltpu.VMEM((2, STATE, rows), bf16),
                        pltpu.VMEM((2, STATE, rows), bf16)],
        compiler_params=params,
        interpret=interpret,
        name="states",
    )(x, value_rim, dy, conv_value, usable_wide, cols, write_rows.T, read_rows.T)

    keeps = lax.all_gather(keep, "ctx")

    def wide(value):
        return jnp.repeat(value, HEAD_DIM)[None, :]

    entering = jnp.zeros_like(fresh)
    leaving = jnp.zeros_like(back)
    ahead_keep = jnp.ones_like(keep)
    behind_keep = jnp.ones_like(keep)
    for j in range(1, reach + 1):
        entering = entering + wide(ahead_keep) * shifted(fresh, "ctx", j)
        leaving = leaving + wide(behind_keep) * shifted(back, "ctx", -j)
        ahead_keep = ahead_keep * keeps[jnp.clip(ctx_place - j, 0, context_count - 1)]
        behind_keep = behind_keep * keeps[jnp.clip(ctx_place + j, 0, context_count - 1)]

    y_local, u_local, dgram = pl.pallas_call(
        local_kernel,
        grid=(pairs,),
        in_specs=[col_spec, col_spec, cols_spec, pl.BlockSpec((1, PAIR, rows), lambda g: (g, 0, 0)),
                  fixed(rows, rows), fixed(rows, rows)],
        out_specs=[col_spec, col_spec, fixed(rows, rows)],
        out_shape=[like(rows, channels), like(rows, channels), like(rows, rows)],
        scratch_shapes=[pltpu.VMEM((2, rows, rows), bf16), pltpu.VMEM((2, rows, rows), bf16)],
        compiler_params=params,
        cost_estimate=pl.CostEstimate(flops=30 * 10**9, bytes_accessed=20 * 10**6, transcendentals=10**7),
        interpret=interpret,
        name="local",
    )(pre, dy, cols, row_form, gram, gram_t)

    mixed, vgrad, tail, rim_grad, tap_grad, token_sums, skip_sums, dproj = pl.pallas_call(
        final_kernel,
        grid=(pairs,),
        in_specs=[col_spec, col_spec, eight_spec, col_spec, cols_spec, fixed(rows, rim * LANES), taps_spec,
                  pl.BlockSpec((1, LANES), lambda g: (0, g)), fixed(rows, 2 * STATE), state_spec, state_spec,
                  col_spec, col_spec],
        out_specs=[col_spec, col_spec, eight_spec, eight_spec, taps_spec,
                   pl.BlockSpec((1, 2 * PAIR, rows), lambda g: (g, 0, 0)),
                   pl.BlockSpec((1, 8, LANES), lambda g: (g, 0, 0)), fixed(rows, 2 * STATE)],
        out_shape=[like(rows, channels, dtype=bf16), like(rows, channels, dtype=bf16), like(8, channels),
                   like(8, channels), like(KERNEL, channels), like(pairs, 2 * PAIR, rows),
                   like(pairs, 8, LANES), like(rows, 2 * STATE)],
        scratch_shapes=[pltpu.VMEM((rows + 8, LANES), f32), pltpu.VMEM((rows + 16, LANES), f32),
                        pltpu.VMEM((2, rows, 2 * STATE), bf16)],
        compiler_params=params,
        interpret=interpret,
        name="final",
    )(pre, x, value_rim, dy, cols, usable_wide, conv_value, wide(skip_gain), projected, entering, leaving,
      y_local, u_local)

    dgram = jnp.where(allowed, dgram, 0.0)
    dread = jnp.dot(dgram, write_rows, precision=precise)
    dwrite = jnp.dot(dgram.T, read_rows, precision=precise)
    dprojected = dproj + jnp.concatenate([dwrite, dread], axis=1)
    dstate, dconv_state, dstate_rim = state_pullback(dprojected)

    sums = token_sums.reshape(pairs, 2, PAIR, rows)
    out_dot = sums[:, 0].reshape(heads, rows)
    in_dot = sums[:, 1].reshape(heads, rows)
    closing = jnp.sum(leaving * (wide(keep) * entering + fresh), axis=0)
    closing = jnp.sum(closing.reshape(heads, HEAD_DIM), axis=1)
    dcum = out_dot - step * in_dot
    order = jnp.arange(rows)
    later = (order[:, None] >= order[None, :]).astype(f32)
    dlog = jnp.dot(dcum, later, precision=precise) + closing[:, None]
    dstep = in_dot - rate * dlog
    step_grad = dstep * jax.nn.sigmoid(logits)
    head_part = jnp.stack([
        jnp.sum(step_grad, axis=1),
        jnp.sum(dlog * log_decay, axis=1),
        jnp.sum(skip_sums[:, 0].reshape(heads, HEAD_DIM), axis=1),
    ])

    rims_back = shifted(jnp.concatenate([rim_grad[8 - rim :], dstate_rim], axis=1), "ctx", -1)
    tail_total = tail.at[8 - rim :].add(rims_back[:, :channels])
    value_grad = lax.dynamic_update_slice(vgrad, tail_total.astype(bf16), (rows - 8, 0))
    state_partial = dstate.at[tail_rows:].add(rims_back[:, channels:])
    state_grad = lax.psum(state_partial, "head").astype(bf16)
    conv_value_grad, head_grads = lax.psum((tap_grad, head_part), ("dp", "ctx"))
    conv_state_grad = lax.psum(dconv_state, ("dp", "ctx", "head"))
    return (
        mixed[None],
        value_grad[None],
        state_grad[None],
        step_grad[None],
        conv_value_grad,
        conv_state_grad,
        head_grads,
    )


def solution(mesh, interpret=False):
    return jax.shard_map(
        partial(on_device, interpret=interpret),
        mesh=mesh,
        in_specs=(
            P("dp", "ctx", "head"),
            P("dp", "ctx", None),
            P("dp", "head", "ctx"),
            P("dp", None),
            P(None, "head"),
            P(),
            P("head"),
            P("head"),
            P("head"),
            P("dp", "ctx", "head"),
        ),
        out_specs=(
            P("dp", "ctx", "head"),
            P("dp", "ctx", "head"),
            P("dp", "ctx", None),
            P("dp", "head", "ctx"),
            P(None, "head"),
            P(),
            P(None, "head"),
        ),
        check_vma=False,
    )
```

time: 666 us -> 246 us (0.37); the launches traced: 657 us -> 245 us
  matrix products: 151 us -> 9.19 us
  waiting for transfers between devices: 130 us -> 10.3 us
  other arithmetic: 107 us -> 9.83 us
  local copies, waits for them, and re-layouts: 109 us -> 19.1 us
  Pallas kernels: 0 us -> 65.2 us
  loops' own time: 36.3 us -> 0 us
  blocking collectives: 99.6 us -> 110 us
    dot_general x31 -> x6, matrix products: 151 us -> 9.19 us  [the longest x1 2.04 us: on_device(): jnp.dot(read_rows, write_rows.T, precision=precise)]
    ppermute x10 -> x6, waiting for transfers between devices: 130 us -> 10.3 us  [shifted(): lax.ppermute(value, axis, [(source, source + steps) for source in range(l...]
    pallas_call x0 -> x3, Pallas kernels: none -> 65.2 us  [the longest x1 24.6 us: on_device(): pl.pallas_call(local_kernel, grid=(pairs,), in_specs=[col_spec, col_spec,...]
    another operation x3 -> x0, loops' own time: 36.3 us -> none  [the longest x2 36.2 us: run_blocks(): lax.scan(jax.checkpoint(one_block), initial, jnp.arange(blocks, dtype=jnp...]
    reduce_sum x9 -> x4, other arithmetic: 28.3 us -> 1.36 us  [the longest x1 0.6 us: causal_conv(): weights[offset][None, :] * padded[offset:offset + length]]
    another operation x24 -> x3, other arithmetic: 22.2 us -> 0.9 us
    another operation x35 -> x5, local copies, waits for them, and re-layouts: 15.9 us -> 0.29 us  [the longest x1 0.08 us: wide(): return jnp.repeat(value, HEAD_DIM)[None, :]]
    reduce_sum x10 -> x0, local copies, waits for them, and re-layouts: 13.5 us -> none  [the longest x4 6.05 us: block_pass(): cumulative[:, :, None] - cumulative[:, None, :]]
  transfers between devices with their start and end apart: 10 -> 6, of which waited for: 6 -> 1; matrix products, arithmetic and copies ran while one was open for 8% -> 9% of each run, Pallas kernels for 0% -> 10%
where the time goes in v1:
time: 246 us; the launch traced here: 245 us
  blocking collectives  110 us (45%)
  Pallas kernels  65.2 us (27%)
  local copies, waits for them, and re-layouts  19.1 us (8%)
  starting transfers between devices  18.2 us (7%)
  waiting for transfers between devices  10.3 us (4%)
  other arithmetic  9.83 us (4%)
  matrix products  9.19 us (4%)
  between operations  2.67 us (1%)
    psum x1, blocking collectives, on_device(): conv_state_grad = lax.psum(dconv_state, ('dp', 'ctx', 'head'))  42.7 us
    psum x1, blocking collectives, on_device(): conv_value_grad, head_grads = lax.psum((tap_grad, head_part), ('dp', 'ctx'))  29.4 us
    psum x1, blocking collectives, on_device(): state_grad = lax.psum(state_partial, 'head').astype(bf16)  29.1 us
    pallas_call x1, Pallas kernels, on_device(): pl.pallas_call(local_kernel, grid=(pairs,), in_specs=[col_spec, col_spec,...  24.6 us
    pallas_call x1, Pallas kernels, on_device(): pl.pallas_call(final_kernel, grid=(pairs,), in_specs=[col_spec, col_spec,...  23.3 us
    ppermute x6, starting transfers between devices, shifted(): lax.ppermute(value, axis, [(source, source + steps) for source in range(l...  18.2 us
    pallas_call x1, Pallas kernels, on_device(): pl.pallas_call(states_kernel, grid=(pairs,), in_specs=[col_spec, eight_sp...  17.4 us
    ppermute x6, waiting for transfers between devices, shifted(): lax.ppermute(value, axis, [(source, source + steps) for source in range(l...  10.3 us
  transfers between devices with their start and end apart: 6, of which 1 were waited for; matrix products, arithmetic and copies ran while one was open for 9% of the time, Pallas kernels for 10%

profile of v1, /device:TPU:0, one launch (start us, length us, event | category | flops | bytes accessed | tf_op | source)
XLA Modules:
  0.0 244.6 jit_solution(5536380352921671407)
XLA Ops:
  2.1 4.8 %collective-permute-start = (bf16[3,2304]{1,0:T(4,128)(2,1)S(1)}, bf16[3,2304]{1,0:T(4,128)(2,1)S(1)}, u32[]{:S(2)}, u32[]{:S(2)}) collective-permute-start(bf16[3,2304]{1,0:T(4,128)(2,1)S(1)} %pad_maximum_fusion.3), channel_id=1, source_target_pairs={{0,4},{4,8},{8,12},{1,5},{5,9},{9,13},{2,6},{6,10},{10,14},{3,7},{... | collective-permute-start | bytes 41480 | tf_op jit(solution)/shard_map/ppermute | solution.py:26
  10.5 1.2 fusion.65
  16.8 1.2 dynamic-slice.16
  18.8 8.9 %all-reduce.9 = f32[128]{0:T(128)S(1)} all-reduce(f32[128]{0:T(128)S(1)} %get-tuple-element.79), channel_id=2, replica_groups=mesh['dp'=2,'ctx'=4,'head'=4] {'ctx'}, use_global_device_ids=true, to_apply=%add.9 | all-reduce | flops 128 | bytes 1024
  31.5 2.7 %copy.56.cols = f32[16,512,12]{2,1,0:T(8,128)} copy(f32[16,512,12]{1,0,2:T(8,128)S(1)} %bitcast.103) | data formatting | bytes 786432 | tf_op jit(solution)/shard_map/reshape | solution.py:307
  34.8 1.2 fusion.12
  36.9 2.0 convolution_select_fusion.1.gram
  38.9 2.0 convolution_select_fusion.gram_t
  41.0 1.8 copy.58.read_t
  42.7 1.8 copy.57.write_t
  46.4 17.4 %states.1 = (f32[512,2048]{1,0:T(8,128)}, f32[128,2048]{1,0:T(8,128)S(1)}, f32[128,2048]{1,0:T(8,128)S(1)}) custom-call(bf16[512,2048]{1,0:T(8,128)(2,1)S(1)} %bitcast.99, f32[8,2048]{1,0:T(8,128)S(1)} %pad_convert_fusion.rim, bf16[512,2048]{1,0:T(8,128)(2,1)} %bitcast.100, f32[4,2048]{1,0:T(4,128)S(1)} %copy-done.6, f32[512,384]{1,0:T(8,128)S(1)} %pad_maximum_fusion.usable, ...), custom_call_target="tpu_custom_call" | custom-call | tf_op jit(solution)/shard_map/states/pallas_call | solution.py:325
  63.8 1.3 collective-permute-start.4
  65.1 1.3 collective-permute-start.3
  66.4 5.3 %collective-permute-start.2 = (f32[128,2048]{1,0:T(8,128)S(1)}, f32[128,2048]{1,0:T(8,128)S(1)}, u32[]{:S(2)}, u32[]{:S(2)}) collective-permute-start(f32[128,2048]{1,0:T(8,128)S(1)} %get-tuple-element.46), channel_id=1, source_target_pairs={{0,8},{4,12},{1,9},{5,13},{2,10},{6,14},{3,11},{7,15},{16,24},{20,... | collective-permute-start | bytes 3145736 | tf_op jit(solution)/shard_map/ppermute | solution.py:26
  71.7 4.2 %collective-permute-start.1 = (f32[128,2048]{1,0:T(8,128)S(1)}, f32[128,2048]{1,0:T(8,128)S(1)}, u32[]{:S(2)}, u32[]{:S(2)}) collective-permute-start(f32[128,2048]{1,0:T(8,128)S(1)} %get-tuple-element.46), channel_id=1, source_target_pairs={{0,4},{4,8},{8,12},{1,5},{5,9},{9,13},{2,6},{6,10},{10,14},{3,7},{... | collective-permute-start | bytes 3145736 | tf_op jit(solution)/shard_map/ppermute | solution.py:26
  76.0 24.6 %local.1 = (f32[512,2048]{1,0:T(8,128)}, f32[512,2048]{1,0:T(8,128)}, f32[512,512]{1,0:T(8,128)S(1)}) custom-call(f32[512,2048]{1,0:T(8,128)} %get-tuple-element.45.pre_ref, bf16[512,2048]{1,0:T(8,128)(2,1)S(1)} %bitcast.102, f32[16,512,12]{2,1,0:T(8,128)} %copy.56.cols, f32[16,2,512]{2,1,0:T(2,128)S(1)} %copy-done.7, f32[512,512]{1,0:T(8,128)S(1)} %copy-done.4, ...), custom_call_target="tpu_custom_call" | custom-call | flops 30000001024 | bytes 20000000 | tf_op jit(solution)/shard_map/local/pallas_call | solution.py:354
  101.6 2.0 fusion.2
  103.6 10.3 %collective-permute-done.2 = f32[128,2048]{1,0:T(8,128)S(1)} collective-permute-done((f32[128,2048]{1,0:T(8,128)S(1)}, f32[128,2048]{1,0:T(8,128)S(1)}, u32[]{:S(2)}, u32[]{:S(2)}) %collective-permute-start.2) | collective-permute-done | bytes 1048608 | tf_op jit(solution)/shard_map/ppermute | solution.py:26
  114.5 23.3 %final.1 = (bf16[512,2048]{1,0:T(8,128)(2,1)}, bf16[512,2048]{1,0:T(8,128)(2,1)}, f32[8,2048]{1,0:T(8,128)S(1)}, f32[8,2048]{1,0:T(8,128)S(1)}, f32[4,2048]{1,0:...) custom-call(f32[512,2048]{1,0:T(8,128)} %get-tuple-element.45.pre_ref, ...), custom_call_target="tpu_custom_call" | custom-call | tf_op jit(solution)/shard_map/final/pallas_call | solution.py:368
  139.8 1.3 collective-permute-start.5
  141.1 1.1 fusion.60
  142.3 42.7 %psum.30 = f32[4,256]{1,0:T(4,128)} all-reduce(f32[4,256]{1,0:T(4,128)S(1)} %pad_add_fusion.2), channel_id=1, replica_groups=mesh['dp'=2,'ctx'=4,'head'=4] {'dp','ctx','head'}, use_global_device_ids=true, to_apply=%region_10.11 | all-reduce | flops 1024 | bytes 8192 | tf_op jit(solution)/shard_map/psum | solution.py:417
  185.0 29.4 %all-reduce.10 = (f32[4,2048]{1,0:T(4,128)}, f32[3,32]{1,0:T(4,128)}) all-reduce(f32[4,2048]{1,0:T(4,128)S(1)} %get-tuple-element.57, f32[3,32]{1,0:T(4,128)S(1)} %pad_maximum_fusion.4), channel_id=1, replica_groups=mesh['dp'=2,'ctx'=4,'head'=4] {'dp','ctx'}, use_global_device_ids=true, to_apply=%region_5.6 | all-reduce | flops 8288 | bytes 66304 | tf_op jit(solution)/shard_map/psum | solution.py:416
  214.5 29.1 %all-reduce.12 = bf16[512,256]{1,0:T(8,128)(2,1)} all-reduce(f32[512,256]{1,0:T(8,128)S(1)} %scatter-add.9), channel_id=1, replica_groups=mesh['dp'=2,'ctx'=4,'head'=4] {'head'}, use_global_device_ids=true, to_apply=%region_2.3 | all-reduce | flops 131072 | bytes 786432 | tf_op jit(solution)/shard_map/psum | solution.py:415
  (149 shorter events, 21.0 us)
Async XLA Ops:
  2.1 32.1 %collective-permute-start = (bf16[3,2304]{1,0:T(4,128)(2,1)S(1)}, bf16[3,2304]{1,0:T(4,128)(2,1)S(1)}, u32[]{:S(2)}, u32[]{:S(2)}) collective-permute-start(bf16[3,2304]{1,0:T(4,128)(2,1)S(1)} %pad_maximum_fusion.3), channel_id=1, source_target_pairs={{0,4},{4,8},{8,12},{1,5},{5,9},{9,13},{2,6},{6,10},{10,14},{3,7},{... | collective-permute-start | bytes 41480 | tf_op jit(solution)/shard_map/ppermute | solution.py:26
  10.5 24.3 %copy-start.14 = (f32[512]{0:T(512)}, f32[512]{0:T(512)S(1)}, u32[]{:S(2)}) copy-start(f32[512]{0:T(512)S(1)} %get-tuple-element.120) | copy-start | bytes 6148
  11.7 17.4 %copy-start.29 = (f32[32]{0:T(128)}, f32[32]{0:T(128)S(1)}, u32[]{:S(2)}) copy-start(f32[32]{0:T(128)S(1)} %get-tuple-element.126) | copy-start | bytes 388
  15.7 19.1 %copy-start.8 = (f32[512,256]{1,0:T(8,128)}, f32[512,256]{1,0:T(8,128)S(1)}, u32[]{:S(2)}) copy-start(f32[512,256]{1,0:T(8,128)S(1)} %bitcast_convert_fusion) | copy-start | bytes 1572868
  15.7 14.6 %copy-start.27 = (f32[32]{0:T(128)S(1)}, f32[32]{0:T(128)}, u32[]{:S(2)}) copy-start(f32[32]{0:T(128)} %param.22) | copy-start | bytes 388
  16.6 18.2 %copy-start.18 = (f32[1,256]{1,0:T(1,128)}, f32[1,256]{1,0:T(1,128)S(1)}, u32[]{:S(2)}) copy-start(f32[1,256]{1,0:T(1,128)S(1)} %get-tuple-element.114) | copy-start | bytes 3076
  16.6 18.2 %copy-start.20 = (f32[1,256]{1,0:T(1,128)}, f32[1,256]{1,0:T(1,128)S(1)}, u32[]{:S(2)}) copy-start(f32[1,256]{1,0:T(1,128)S(1)} %get-tuple-element.115) | copy-start | bytes 3076
  16.6 18.2 %copy-start.22 = (f32[1,256]{1,0:T(1,128)}, f32[1,256]{1,0:T(1,128)S(1)}, u32[]{:S(2)}) copy-start(f32[1,256]{1,0:T(1,128)S(1)} %get-tuple-element.116) | copy-start | bytes 3076
  16.6 18.2 %copy-start.24 = (f32[1,256]{1,0:T(1,128)}, f32[1,256]{1,0:T(1,128)S(1)}, u32[]{:S(2)}) copy-start(f32[1,256]{1,0:T(1,128)S(1)} %get-tuple-element.117) | copy-start | bytes 3076
  36.8 7.7 %copy-start.6 = (f32[4,2048]{1,0:T(4,128)S(1)}, f32[4,2048]{1,0:T(4,128)}, u32[]{:S(2)}) copy-start(f32[4,2048]{1,0:T(4,128)} %taps.3) | copy-start | bytes 98308
  46.4 29.5 %copy-start.1 = (bf16[1,512,2048]{2,1,0:T(8,128)(2,1)S(1)}, bf16[1,512,2048]{2,1,0:T(8,128)(2,1)}, u32[]{:S(2)}) copy-start(bf16[1,512,2048]{2,1,0:T(8,128)(2,1)} %param.23) | copy-start | bytes 6291460
  46.4 29.5 %copy-start.4 = (f32[512,512]{1,0:T(8,128)S(1)}, f32[512,512]{1,0:T(8,128)}, u32[]{:S(2)}) copy-start(f32[512,512]{1,0:T(8,128)} %convolution_select_fusion.1.gram) | copy-start | bytes 3145732
  46.4 29.5 %copy-start.5 = (f32[512,512]{1,0:T(8,128)S(1)}, f32[512,512]{1,0:T(8,128)}, u32[]{:S(2)}) copy-start(f32[512,512]{1,0:T(8,128)} %convolution_select_fusion.gram_t) | copy-start | bytes 3145732
  46.4 29.5 %copy-start.7 = (f32[16,2,512]{2,1,0:T(2,128)S(1)}, f32[16,2,512]{2,1,0:T(2,128)}, u32[]{:S(2)}) copy-start(f32[16,2,512]{2,1,0:T(2,128)} %mul.327.rows_ref) | copy-start | bytes 196612
  63.8 39.8 %collective-permute-start.4 = (f32[128,2048]{1,0:T(8,128)S(1)}, f32[128,2048]{1,0:T(8,128)S(1)}, u32[]{:S(2)}, u32[]{:S(2)}) collective-permute-start(f32[128,2048]{1,0:T(8,128)S(1)} %get-tuple-element.47), channel_id=1, source_target_pairs={{8,0},{12,4},{9,1},{13,5},{10,2},{14,6},{11,3},{15,7},{24,16},{28,... | collective-permute-start | bytes 3145736 | tf_op jit(solution)/shard_map/ppermute | solution.py:26
  65.1 38.5 %collective-permute-start.3 = (f32[128,2048]{1,0:T(8,128)S(1)}, f32[128,2048]{1,0:T(8,128)S(1)}, u32[]{:S(2)}, u32[]{:S(2)}) collective-permute-start(f32[128,2048]{1,0:T(8,128)S(1)} %get-tuple-element.47), channel_id=1, source_target_pairs={{4,0},{8,4},{12,8},{5,1},{9,5},{13,9},{6,2},{10,6},{14,10},{7,3},{... | collective-permute-start | bytes 3145736 | tf_op jit(solution)/shard_map/ppermute | solution.py:26
  66.4 47.5 %collective-permute-start.2 = (f32[128,2048]{1,0:T(8,128)S(1)}, f32[128,2048]{1,0:T(8,128)S(1)}, u32[]{:S(2)}, u32[]{:S(2)}) collective-permute-start(f32[128,2048]{1,0:T(8,128)S(1)} %get-tuple-element.46), channel_id=1, source_target_pairs={{0,8},{4,12},{1,9},{5,13},{2,10},{6,14},{3,11},{7,15},{16,24},{20,... | collective-permute-start | bytes 3145736 | tf_op jit(solution)/shard_map/ppermute | solution.py:26
  71.7 42.2 %collective-permute-start.1 = (f32[128,2048]{1,0:T(8,128)S(1)}, f32[128,2048]{1,0:T(8,128)S(1)}, u32[]{:S(2)}, u32[]{:S(2)}) collective-permute-start(f32[128,2048]{1,0:T(8,128)S(1)} %get-tuple-element.46), channel_id=1, source_target_pairs={{0,4},{4,8},{8,12},{1,5},{5,9},{9,13},{2,6},{6,10},{10,14},{3,7},{... | collective-permute-start | bytes 3145736 | tf_op jit(solution)/shard_map/ppermute | solution.py:26
  100.6 13.4 %copy-start.13 = (f32[2048]{0:T(1024)S(1)}, f32[2048]{0:T(1024)}, u32[]{:S(2)}) copy-start(f32[2048]{0:T(1024)} %mul.344) | copy-start | bytes 24580
  114.5 23.4 %copy-start.9 = (f32[512,256]{1,0:T(8,128)S(1)}, f32[512,256]{1,0:T(8,128)}, u32[]{:S(2)}) copy-start(f32[512,256]{1,0:T(8,128)} %copy-done.8) | copy-start | bytes 1572868
  114.5 23.4 %copy-start.10 = (f32[512,256]{1,0:T(8,128)S(1)}, f32[512,256]{1,0:T(8,128)}, u32[]{:S(2)}) copy-start(f32[512,256]{1,0:T(8,128)} %get-tuple-element.82) | copy-start | bytes 1572868
  114.5 23.4 %copy-start.11 = (bf16[1,512,256]{2,1,0:T(8,128)(2,1)S(1)}, bf16[1,512,256]{2,1,0:T(8,128)(2,1)}, u32[]{:S(2)}) copy-start(bf16[1,512,256]{2,1,0:T(8,128)(2,1)} %param.15) | copy-start | bytes 786436
  114.5 23.4 %copy-start.15 = (f32[512]{0:T(512)S(1)}, f32[512]{0:T(512)}, u32[]{:S(2)}) copy-start(f32[512]{0:T(512)} %copy-done.14) | copy-start | bytes 6148
  139.8 74.6 %collective-permute-start.5 = (f32[3,2304]{1,0:T(4,128)S(1)}, f32[3,2304]{1,0:T(4,128)S(1)}, u32[]{:S(2)}, u32[]{:S(2)}) collective-permute-start(f32[3,2304]{1,0:T(4,128)S(1)} %pad_maximum_fusion.2), channel_id=1, source_target_pairs={{4,0},{8,4},{12,8},{5,1},{9,5},{13,9},{6,2},{10,6},{14,10},{7,3},{... | collective-permute-start | bytes 82952 | tf_op jit(solution)/shard_map/ppermute | solution.py:26
  (13 other events, 26.6 us)

commit v2 on v1

--- a/solution.py
+++ b/solution.py
@@ -81,7 +81,7 @@
     return 1.0 / (1.0 + jnp.exp(-value))
 
 
-def states_kernel(x, rim, dy, taps, usable, cols, write_t, read_t, pre_out, fresh, back, pad, wt_s, rt_s):
+def states_kernel(x, rim, dy, taps, usable, cols, write_t, read_t, keep, pre_out, fresh, back, pad, wt_s, rt_s):
     rows = x.shape[0]
 
     @pl.when(pl.program_id(0) == 0)
@@ -100,9 +100,11 @@
     pre_out[...] = pre
     columns = cols[0]
     weighted = pre * sigmoid(pre) * (spread(columns, C_STEP) * spread(columns, C_LEAVE))
-    fresh[...] = mm3((wt_s[0], wt_s[1]), split(weighted))
+    fresh[:STATE] = mm3((wt_s[0], wt_s[1]), split(weighted))
+    fresh[STATE:] = jnp.broadcast_to(keep[...], (8, LANES))
     grad = dy[...].astype(f32) * spread(columns, C_ENTER)
-    back[...] = mm3((rt_s[0], rt_s[1]), split(grad))
+    back[:STATE] = mm3((rt_s[0], rt_s[1]), split(grad))
+    back[STATE:] = jnp.broadcast_to(keep[...], (8, LANES))
 
 
 def local_kernel(pre_ref, dy, cols, rows_ref, gram, gram_t, y_out, u_out, dgram, g_s, gt_s):
@@ -226,6 +228,108 @@
     tail[...] = total[rows:]
 
 
+def sum_kernel(
+    groups, members, local_rows, part, small, state_out, small_out, cs_out,
+    part_in, small_in, chunk, chunk_in, cs_in, send_p, recv_p, send_s, recv_s, send_c, recv_c, send_k, recv_k,
+):
+    ctx = lax.axis_size("ctx")
+    me = lax.axis_index("head")
+    mine = lax.axis_index("dp") * ctx + lax.axis_index("ctx")
+    size = part.shape[0] // groups
+
+    def along(offset):
+        return {"head": lax.rem(me + offset, groups)}
+
+    def beside(offset):
+        other = lax.rem(mine + offset, members)
+        return {"dp": other // ctx, "ctx": lax.rem(other, ctx)}
+
+    def remote(src, dst, send, recv, device):
+        return pltpu.make_async_remote_copy(
+            src_ref=src, dst_ref=dst, send_sem=send, recv_sem=recv, device_id=device,
+            device_id_type=pl.DeviceIdType.MESH,
+        )
+
+    barrier = pltpu.get_barrier_semaphore()
+    for o in range(1, groups):
+        pl.semaphore_signal(barrier, inc=1, device_id=along(o), device_id_type=pl.DeviceIdType.MESH)
+    for o in range(1, members):
+        pl.semaphore_signal(barrier, inc=1, device_id=beside(o), device_id_type=pl.DeviceIdType.MESH)
+    pl.semaphore_wait(barrier, groups + members - 2)
+
+    first = []
+    for o in range(1, groups):
+        to = lax.rem(me + o, groups)
+        src = part.at[pl.ds(pl.multiple_of(to * size, size), size)]
+        first.append(remote(src, part_in.at[o - 1], send_p.at[o - 1], recv_p.at[o - 1], along(o)))
+    for o in range(1, members):
+        first.append(remote(small, small_in.at[o - 1], send_s.at[o - 1], recv_s.at[o - 1], beside(o)))
+    for copy in first:
+        copy.start()
+    for copy in first:
+        copy.wait()
+
+    total = part[pl.ds(pl.multiple_of(me * size, size), size), :]
+    for o in range(1, groups):
+        total = total + part_in[o - 1]
+    chunk[...] = total.astype(bf16)
+
+    def in_order(own, slots, place, count):
+        result = None
+        for s in range(count):
+            slot = jnp.maximum(lax.rem(place - s + count, count) - 1, 0)
+            term = jnp.where(place == s, own, slots[slot])
+            result = term if result is None else result + term
+        return result
+
+    summed = in_order(small[...], small_in, mine, members)
+    small_out[...] = summed[:local_rows]
+    cs_out[...] = summed[local_rows:]
+    second = []
+    for o in range(1, groups):
+        second.append(remote(chunk, chunk_in.at[o - 1], send_c.at[o - 1], recv_c.at[o - 1], along(o)))
+        second.append(remote(cs_out, cs_in.at[o - 1], send_k.at[o - 1], recv_k.at[o - 1], along(o)))
+    for copy in second:
+        copy.start()
+    state_out[pl.ds(pl.multiple_of(me * size, size), size), :] = chunk[...]
+    for copy in second:
+        copy.wait()
+    for o in range(1, groups):
+        origin = lax.rem(me - o + groups, groups)
+        state_out[pl.ds(pl.multiple_of(origin * size, size), size), :] = chunk_in[o - 1]
+    cs_out[...] = in_order(cs_out[...], cs_in, me, groups)
+
+
+def sum_across(part, small, local_rows):
+    groups = lax.axis_size("head")
+    members = lax.axis_size("dp") * lax.axis_size("ctx")
+    rows, width = part.shape
+    extra = small.shape[0] - local_rows
+    size = rows // groups
+    vmem = pl.BlockSpec(memory_space=pltpu.VMEM)
+    dma = pltpu.SemaphoreType.DMA
+    return pl.pallas_call(
+        partial(sum_kernel, groups, members, local_rows),
+        in_specs=[vmem, vmem],
+        out_specs=[vmem, vmem, vmem],
+        out_shape=[jax.ShapeDtypeStruct((rows, width), bf16), jax.ShapeDtypeStruct((local_rows, 128), f32),
+                   jax.ShapeDtypeStruct((extra, 128), f32)],
+        scratch_shapes=[
+            pltpu.VMEM((groups - 1, size, width), f32),
+            pltpu.VMEM((members - 1, *small.shape), f32),
+            pltpu.VMEM((size, width), bf16),
+            pltpu.VMEM((groups - 1, size, width), bf16),
+            pltpu.VMEM((groups - 1, extra, 128), f32),
+            dma((groups - 1,)), dma((groups - 1,)), dma((members - 1,)), dma((members - 1,)),
+            dma((groups - 1,)), dma((groups - 1,)), dma((groups - 1,)), dma((groups - 1,)),
+        ],
+        compiler_params=pltpu.CompilerParams(
+            collective_id=0, has_side_effects=True, vmem_limit_bytes=32 * 1024 * 1024
+        ),
+        name="sums",
+    )(part, small)
+
+
 def on_device(
     value_input,
     state_proj,
@@ -311,7 +415,12 @@
     cols_spec = pl.BlockSpec((1, rows, 6 * PAIR), lambda g: (g, 0, 0))
     eight_spec = pl.BlockSpec((8, LANES), lambda g: (0, g))
     taps_spec = pl.BlockSpec((KERNEL, LANES), lambda g: (0, g))
+    one_spec = pl.BlockSpec((1, LANES), lambda g: (0, g))
+    sent_spec = pl.BlockSpec((STATE + 8, LANES), lambda g: (0, g))
     state_spec = pl.BlockSpec((STATE, LANES), lambda g: (0, g))
+
+    def wide(value):
+        return jnp.repeat(value, HEAD_DIM)[None, :]
 
     def fixed(*shape):
         return pl.BlockSpec(shape, lambda g: (0,) * len(shape))
@@ -326,30 +435,24 @@
         states_kernel,
         grid=(pairs,),
         in_specs=[col_spec, eight_spec, col_spec, taps_spec, fixed(rows, rim * LANES), cols_spec,
-                  fixed(STATE, rows), fixed(STATE, rows)],
-        out_specs=[col_spec, state_spec, state_spec],
-        out_shape=[like(rows, channels), like(STATE, channels), like(STATE, channels)],
+                  fixed(STATE, rows), fixed(STATE, rows), one_spec],
+        out_specs=[col_spec, sent_spec, sent_spec],
+        out_shape=[like(rows, channels), like(STATE + 8, channels), like(STATE + 8, channels)],
         scratch_shapes=[pltpu.VMEM((rows + 8, LANES), f32), pltpu.VMEM((2, STATE, rows), bf16),
                         pltpu.VMEM((2, STATE, rows), bf16)],
         compiler_params=params,
         interpret=interpret,
         name="states",
-    )(x, value_rim, dy, conv_value, usable_wide, cols, write_rows.T, read_rows.T)
-
-    keeps = lax.all_gather(keep, "ctx")
-
-    def wide(value):
-        return jnp.repeat(value, HEAD_DIM)[None, :]
-
-    entering = jnp.zeros_like(fresh)
-    leaving = jnp.zeros_like(back)
-    ahead_keep = jnp.ones_like(keep)
-    behind_keep = jnp.ones_like(keep)
+    )(x, value_rim, dy, conv_value, usable_wide, cols, write_rows.T, read_rows.T, wide(keep))
+
+    entering, leaving = jnp.zeros((2, STATE, channels), f32)
+    ahead_keep, behind_keep = jnp.ones((2, 1, channels), f32)
     for j in range(1, reach + 1):
-        entering = entering + wide(ahead_keep) * shifted(fresh, "ctx", j)
-        leaving = leaving + wide(behind_keep) * shifted(back, "ctx", -j)
-        ahead_keep = ahead_keep * keeps[jnp.clip(ctx_place - j, 0, context_count - 1)]
-        behind_keep = behind_keep * keeps[jnp.clip(ctx_place + j, 0, context_count - 1)]
+        ahead, behind = shifted(fresh, "ctx", j), shifted(back, "ctx", -j)
+        entering = entering + ahead_keep * ahead[:STATE]
+        leaving = leaving + behind_keep * behind[:STATE]
+        ahead_keep = ahead_keep * ahead[STATE : STATE + 1]
+        behind_keep = behind_keep * behind[STATE : STATE + 1]
 
     y_local, u_local, dgram = pl.pallas_call(
         local_kernel,
@@ -394,7 +497,7 @@
     sums = token_sums.reshape(pairs, 2, PAIR, rows)
     out_dot = sums[:, 0].reshape(heads, rows)
     in_dot = sums[:, 1].reshape(heads, rows)
-    closing = jnp.sum(leaving * (wide(keep) * entering + fresh), axis=0)
+    closing = jnp.sum(leaving * (wide(keep) * entering + fresh[:STATE]), axis=0)
     closing = jnp.sum(closing.reshape(heads, HEAD_DIM), axis=1)
     dcum = out_dot - step * in_dot
     order = jnp.arange(rows)
@@ -412,9 +515,13 @@
     tail_total = tail.at[8 - rim :].add(rims_back[:, :channels])
     value_grad = lax.dynamic_update_slice(vgrad, tail_total.astype(bf16), (rows - 8, 0))
     state_partial = dstate.at[tail_rows:].add(rims_back[:, channels:])
-    state_grad = lax.psum(state_partial, "head").astype(bf16)
-    conv_value_grad, head_grads = lax.psum((tap_grad, head_part), ("dp", "ctx"))
-    conv_state_grad = lax.psum(dconv_state, ("dp", "ctx", "head"))
+    tap_rows = KERNEL * channels // 128
+    head_flat = jnp.pad(head_part.reshape(-1), (0, 8 * 128 - 3 * heads)).reshape(8, 128)
+    small = jnp.concatenate([tap_grad.reshape(tap_rows, 128), head_flat, dconv_state.reshape(-1, 128)])
+    state_grad, small_sum, conv_state_sum = sum_across(state_partial, small, tap_rows + 8)
+    conv_value_grad = small_sum[:tap_rows].reshape(KERNEL, channels)
+    head_grads = small_sum[tap_rows:].reshape(-1)[: 3 * heads].reshape(3, heads)
+    conv_state_grad = conv_state_sum.reshape(KERNEL, 2 * STATE)
     return (
         mixed[None],
         value_grad[None],

time: 246 us -> 171 us (0.70)
  blocking collectives: 110 us -> 0 us
  Pallas kernels: 65.2 us -> 88 us
  waiting for transfers between devices: 10.3 us -> 18.9 us
    psum x3 -> x0, blocking collectives: 101 us -> none  [the longest x1 42.7 us: on_device(): conv_state_grad = lax.psum(dconv_state, ('dp', 'ctx', 'head'))]
    pallas_call x0 -> x1, Pallas kernels: none -> 22.6 us  [sum_across(): pl.pallas_call(partial(sum_kernel, groups, members, local_rows), in_specs...]
    unnamed x1 -> x0, blocking collectives: 8.93 us -> none
    ppermute x6, waiting for transfers between devices: 10.3 us -> 18.9 us  [shifted(): lax.ppermute(value, axis, [(source, source + steps) for source in range(l...]
  transfers between devices with their start and end apart: 6 -> 6, of which waited for: 1 -> 2; matrix products, arithmetic and copies ran while one was open for 9% -> 10% of each run, Pallas kernels for 10% -> 15%
where the time goes in v2:
time: 171 us; the launch traced here: 169 us
  Pallas kernels  88 us (51%)
  local copies, waits for them, and re-layouts  20.2 us (12%)
  starting transfers between devices  19.2 us (11%)
  waiting for transfers between devices  18.9 us (11%)
  other arithmetic  11.6 us (7%)
  matrix products  9.18 us (5%)
  between operations  2.02 us (1%)
    pallas_call x1, Pallas kernels, on_device(): pl.pallas_call(local_kernel, grid=(pairs,), in_specs=[col_spec, col_spec,...  24.6 us
    pallas_call x1, Pallas kernels, on_device(): pl.pallas_call(final_kernel, grid=(pairs,), in_specs=[col_spec, col_spec,...  23.3 us
    pallas_call x1, Pallas kernels, sum_across(): pl.pallas_call(partial(sum_kernel, groups, members, local_rows), in_specs...  22.6 us
    ppermute x6, starting transfers between devices, shifted(): lax.ppermute(value, axis, [(source, source + steps) for source in range(l...  19.2 us
    ppermute x6, waiting for transfers between devices, shifted(): lax.ppermute(value, axis, [(source, source + steps) for source in range(l...  18.9 us
    pallas_call x1, Pallas kernels, on_device(): pl.pallas_call(states_kernel, grid=(pairs,), in_specs=[col_spec, eight_sp...  17.5 us
    transpose x3, local copies, waits for them, and re-layouts, on_device(): pre, fresh, back = pl.pallas_call(states_kernel, grid=(pairs,), in_specs=...  4.38 us
    unnamed x65, local copies, waits for them, and re-layouts  3.97 us
  transfers between devices with their start and end apart: 6, of which 2 were waited for; matrix products, arithmetic and copies ran while one was open for 10% of the time, Pallas kernels for 15%

profile of v2, /device:TPU:0, one launch (start us, length us, event | category | flops | bytes accessed | tf_op | source)
XLA Modules:
  0.0 169.0 jit_solution(7924581182016553869)
XLA Ops:
  2.1 4.8 %collective-permute-start = (bf16[3,2304]{1,0:T(4,128)(2,1)S(1)}, bf16[3,2304]{1,0:T(4,128)(2,1)S(1)}, u32[]{:S(2)}, u32[]{:S(2)}) collective-permute-start(bf16[3,2304]{1,0:T(4,128)(2,1)S(1)} %pad_maximum_fusion.4), channel_id=1, source_target_pairs={{0,4},{4,8},{8,12},{1,5},{5,9},{9,13},{2,6},{6,10},{10,14},{3,7},{... | collective-permute-start | bytes 41480 | tf_op jit(solution)/shard_map/ppermute | solution.py:26
  10.5 1.1 fusion.66
  14.6 1.0 bitcast_convert_fusion
  19.5 2.7 %copy.56.cols = f32[16,512,12]{2,1,0:T(8,128)} copy(f32[16,512,12]{1,0,2:T(8,128)S(1)} %bitcast.100) | data formatting | bytes 786432 | tf_op jit(solution)/shard_map/reshape | solution.py:411
  22.8 1.2 fusion.14
  24.8 2.0 %convolution_select_fusion.1.gram = f32[512,512]{1,0:T(8,128)} fusion(s32[512]{0:T(512)S(1)} %iota_add_fusion, s32[512]{0:T(512)S(1)} %select_reduce_fusion, f32[512,256]{1,0:T(8,128)S(1)} %get-tuple-element.83.projected), kind=kOutput, calls=%fused_computation.1 | convolution fusion | flops 403701760 | bytes 1579008 | tf_op jit(solution)/shard_map/dot_general | solution.py:376
  26.9 2.0 %convolution_select_fusion.gram_t = f32[512,512]{1,0:T(8,128)} fusion(s32[512]{0:T(512)S(1)} %select_reduce_fusion, s32[512]{0:T(512)S(1)} %iota_add_fusion, f32[512,256]{1,0:T(8,128)S(1)} %get-tuple-element.83.projected), kind=kOutput, calls=%fused_computation | convolution fusion | flops 403701760 | bytes 1579008 | tf_op jit(solution)/shard_map/dot_general | solution.py:377
  28.9 1.8 %copy.58.read_t = f32[128,512]{1,0:T(8,128)} copy(f32[128,512]{0,1:T(8,128)} %get-tuple-element.89) | data formatting | bytes 524288 | tf_op jit(solution)/shard_map/transpose | solution.py:446
  30.7 1.8 %copy.57.write_t = f32[128,512]{1,0:T(8,128)} copy(f32[128,512]{0,1:T(8,128)} %get-tuple-element.90) | data formatting | bytes 524288 | tf_op jit(solution)/shard_map/transpose | solution.py:446
  34.4 17.5 %states.1 = (f32[512,2048]{1,0:T(8,128)}, f32[136,2048]{1,0:T(8,128)S(1)}, f32[136,2048]{1,0:T(8,128)S(1)}) custom-call(bf16[512,2048]{1,0:T(8,128)(2,1)S(1)} %bitcast.95, f32[8,2048]{1,0:T(8,128)S(1)} %pad_convert_fusion.rim, bf16[512,2048]{1,0:T(8,128)(2,1)} %bitcast.96, f32[4,2048]{1,0:T(4,128)S(1)} %copy-done.6, f32[512,384]{1,0:T(8,128)S(1)} %pad_maximum_fusion.usable, ...), custom_call_target="tpu_custom_call" | custom-call | tf_op jit(solution)/shard_map/states/pallas_call | solution.py:434
  52.0 1.3 collective-permute-start.4
  53.2 1.3 collective-permute-start.3
  54.5 6.5 %collective-permute-start.2 = (f32[136,2048]{1,0:T(8,128)S(1)}, f32[136,2048]{1,0:T(8,128)}, u32[]{:S(2)}, u32[]{:S(2)}) collective-permute-start(f32[136,2048]{1,0:T(8,128)S(1)} %get-tuple-element.49), channel_id=1, source_target_pairs={{0,8},{4,12},{1,9},{5,13},{2,10},{6,14},{3,11},{7,15},{16,24},{20,... | collective-permute-start | bytes 3342344 | tf_op jit(solution)/shard_map/ppermute | solution.py:26
  61.0 4.0 %collective-permute-start.1 = (f32[136,2048]{1,0:T(8,128)S(1)}, f32[136,2048]{1,0:T(8,128)S(1)}, u32[]{:S(2)}, u32[]{:S(2)}) collective-permute-start(f32[136,2048]{1,0:T(8,128)S(1)} %get-tuple-element.49), channel_id=1, source_target_pairs={{0,4},{4,8},{8,12},{1,5},{5,9},{9,13},{2,6},{6,10},{10,14},{3,7},{... | collective-permute-start | bytes 3342344 | tf_op jit(solution)/shard_map/ppermute | solution.py:26
  65.1 24.6 %local.1 = (f32[512,2048]{1,0:T(8,128)}, f32[512,2048]{1,0:T(8,128)}, f32[512,512]{1,0:T(8,128)S(1)}) custom-call(f32[512,2048]{1,0:T(8,128)} %get-tuple-element.48.pre_ref, bf16[512,2048]{1,0:T(8,128)(2,1)S(1)} %bitcast.98, f32[16,512,12]{2,1,0:T(8,128)} %copy.56.cols, f32[16,2,512]{2,1,0:T(2,128)S(1)} %copy-done.7, f32[512,512]{1,0:T(8,128)S(1)} %copy-done.4, ...), custom_call_target="tpu_custom_call" | custom-call | flops 30000001024 | bytes 20000000 | tf_op jit(solution)/shard_map/local/pallas_call | solution.py:457
  89.6 1.1 fusion.2
  90.7 2.0 %fusion.4 = f32[512,128]{1,0:T(8,128)S(1)} fusion(f32[512,512]{1,0:T(8,128)S(1)} %get-tuple-element.58, s32[512]{0:T(512)S(1)} %iota_add_fusion, s32[512]{0:T(512)S(1)} %select_reduce_fusion, f32[512,256]{1,0:T(8,128)S(1)} %get-tuple-element.83.projected), kind=kOutput, calls=%fused_computation.12 | convolution fusion | flops 403701760 | bytes 1579008 | tf_op jit(solution)/shard_map/dot_general | solution.py:493
  92.8 14.4 %collective-permute-done.2 = f32[136,2048]{1,0:T(8,128)} collective-permute-done((f32[136,2048]{1,0:T(8,128)S(1)}, f32[136,2048]{1,0:T(8,128)}, u32[]{:S(2)}, u32[]{:S(2)}) %collective-permute-start.2) | collective-permute-done | bytes 1114144 | tf_op jit(solution)/shard_map/ppermute | solution.py:26
  107.1 1.7 %multiply_reduce_fusion = (f32[2048]{0:T(1024)S(1)}, f32[128,2048]{1,0:T(8,128)S(1)}, f32[128,2048]{1,0:T(8,128)S(1)}) fusion(f32[136,2048]{1,0:T(8,128)S(1)} %get-tuple-element.49, f32[2048]{0:T(1024)S(1)} %mul.331, f32[136,2048]{1,0:T(8,128)S(1)} %collective-permute-done.4, f32[2048]{0:T(1024)S(1)} %bitcast.110, f32[136,2048]{1,0:T(8,128)S(1)} %collective-permute-done.3, ...), kind=kLoop, calls=%fused_computation.7 | loop fusion | flops 2095104 | bytes 7372800 | tf_op jit(solution)/shard_map/reduce_sum | solution.py:500
  108.9 23.3 %final.1 = (bf16[512,2048]{1,0:T(8,128)(2,1)}, bf16[512,2048]{1,0:T(8,128)(2,1)}, f32[8,2048]{1,0:T(8,128)S(1)}, f32[8,2048]{1,0:T(8,128)S(1)}, f32[4,2048]{1,0:...) custom-call(f32[512,2048]{1,0:T(8,128)} %get-tuple-element.48.pre_ref, ...), custom_call_target="tpu_custom_call" | custom-call | tf_op jit(solution)/shard_map/final/pallas_call | solution.py:471
  134.2 1.1 fusion.59
  135.5 1.3 collective-permute-start.5
  136.9 4.5 %collective-permute-done.5 = f32[3,2304]{1,0:T(4,128)S(1)} collective-permute-done((f32[3,2304]{1,0:T(4,128)S(1)}, f32[3,2304]{1,0:T(4,128)S(1)}, u32[]{:S(2)}, u32[]{:S(2)}) %collective-permute-start.5) | collective-permute-done | bytes 27680 | tf_op jit(solution)/shard_map/ppermute | solution.py:26
  142.1 22.6 %sums.1 = (bf16[512,256]{1,0:T(8,128)(2,1)S(1)}, f32[72,128]{1,0:T(8,128)S(1)}, f32[8,128]{1,0:T(8,128)S(1)}) custom-call(f32[512,256]{1,0:T(8,128)S(1)} %scatter-add.9.part, f32[80,128]{1,0:T(8,128)S(1)} %pad_maximum_fusion.2.small), custom_call_target="tpu_custom_call" | custom-call | tf_op jit(solution)/shard_map/sums/pallas_call | solution.py:311
  (152 shorter events, 21.4 us)
Async XLA Ops:
  2.1 20.1 %collective-permute-start = (bf16[3,2304]{1,0:T(4,128)(2,1)S(1)}, bf16[3,2304]{1,0:T(4,128)(2,1)S(1)}, u32[]{:S(2)}, u32[]{:S(2)}) collective-permute-start(bf16[3,2304]{1,0:T(4,128)(2,1)S(1)} %pad_maximum_fusion.4), channel_id=1, source_target_pairs={{0,4},{4,8},{8,12},{1,5},{5,9},{9,13},{2,6},{6,10},{10,14},{3,7},{... | collective-permute-start | bytes 41480 | tf_op jit(solution)/shard_map/ppermute | solution.py:26
  10.5 12.3 %copy-start.14 = (f32[512]{0:T(512)}, f32[512]{0:T(512)S(1)}, u32[]{:S(2)}) copy-start(f32[512]{0:T(512)S(1)} %get-tuple-element.121) | copy-start | bytes 6148
  15.6 7.2 %copy-start.8 = (f32[512,256]{1,0:T(8,128)}, f32[512,256]{1,0:T(8,128)S(1)}, u32[]{:S(2)}) copy-start(f32[512,256]{1,0:T(8,128)S(1)} %bitcast_convert_fusion) | copy-start | bytes 1572868
  16.5 6.3 %copy-start.18 = (f32[1,256]{1,0:T(1,128)}, f32[1,256]{1,0:T(1,128)S(1)}, u32[]{:S(2)}) copy-start(f32[1,256]{1,0:T(1,128)S(1)} %get-tuple-element.116) | copy-start | bytes 3076
  16.5 6.3 %copy-start.20 = (f32[1,256]{1,0:T(1,128)}, f32[1,256]{1,0:T(1,128)S(1)}, u32[]{:S(2)}) copy-start(f32[1,256]{1,0:T(1,128)S(1)} %get-tuple-element.117) | copy-start | bytes 3076
  16.5 6.3 %copy-start.22 = (f32[1,256]{1,0:T(1,128)}, f32[1,256]{1,0:T(1,128)S(1)}, u32[]{:S(2)}) copy-start(f32[1,256]{1,0:T(1,128)S(1)} %get-tuple-element.118) | copy-start | bytes 3076
  16.5 6.3 %copy-start.24 = (f32[1,256]{1,0:T(1,128)}, f32[1,256]{1,0:T(1,128)S(1)}, u32[]{:S(2)}) copy-start(f32[1,256]{1,0:T(1,128)S(1)} %get-tuple-element.119) | copy-start | bytes 3076
  16.5 2.8 %copy-start.27 = (f32[32]{0:T(128)S(1)}, f32[32]{0:T(128)}, u32[]{:S(2)}) copy-start(f32[32]{0:T(128)} %param.22) | copy-start | bytes 388
  24.0 4.9 %copy-start.17 = (bf16[3,2304]{1,0:T(4,128)(2,1)S(1)}, bf16[3,2304]{1,0:T(4,128)(2,1)}, u32[]{:S(2)}) copy-start(bf16[3,2304]{1,0:T(4,128)(2,1)} %copy-done.16) | copy-start | bytes 41476
  24.8 7.7 %copy-start = (bf16[1,512,2048]{2,1,0:T(8,128)(2,1)S(1)}, bf16[1,512,2048]{2,1,0:T(8,128)(2,1)}, u32[]{:S(2)}) copy-start(bf16[1,512,2048]{2,1,0:T(8,128)(2,1)} %param.14) | copy-start | bytes 6291460
  24.8 7.7 %copy-start.6 = (f32[4,2048]{1,0:T(4,128)S(1)}, f32[4,2048]{1,0:T(4,128)}, u32[]{:S(2)}) copy-start(f32[4,2048]{1,0:T(4,128)} %taps.3) | copy-start | bytes 98308
  34.4 30.6 %copy-start.1 = (bf16[1,512,2048]{2,1,0:T(8,128)(2,1)S(1)}, bf16[1,512,2048]{2,1,0:T(8,128)(2,1)}, u32[]{:S(2)}) copy-start(bf16[1,512,2048]{2,1,0:T(8,128)(2,1)} %param.23) | copy-start | bytes 6291460
  34.4 30.6 %copy-start.4 = (f32[512,512]{1,0:T(8,128)S(1)}, f32[512,512]{1,0:T(8,128)}, u32[]{:S(2)}) copy-start(f32[512,512]{1,0:T(8,128)} %convolution_select_fusion.1.gram) | copy-start | bytes 3145732
  34.4 30.6 %copy-start.5 = (f32[512,512]{1,0:T(8,128)S(1)}, f32[512,512]{1,0:T(8,128)}, u32[]{:S(2)}) copy-start(f32[512,512]{1,0:T(8,128)} %convolution_select_fusion.gram_t) | copy-start | bytes 3145732
  34.4 30.6 %copy-start.7 = (f32[16,2,512]{2,1,0:T(2,128)S(1)}, f32[16,2,512]{2,1,0:T(2,128)}, u32[]{:S(2)}) copy-start(f32[16,2,512]{2,1,0:T(2,128)} %mul.316.rows_ref) | copy-start | bytes 196612
  52.0 40.8 %collective-permute-start.4 = (f32[136,2048]{1,0:T(8,128)S(1)}, f32[136,2048]{1,0:T(8,128)S(1)}, u32[]{:S(2)}, u32[]{:S(2)}) collective-permute-start(f32[136,2048]{1,0:T(8,128)S(1)} %get-tuple-element.50), channel_id=1, source_target_pairs={{8,0},{12,4},{9,1},{13,5},{10,2},{14,6},{11,3},{15,7},{24,16},{28,... | collective-permute-start | bytes 3342344 | tf_op jit(solution)/shard_map/ppermute | solution.py:26
  53.2 39.4 %collective-permute-start.3 = (f32[136,2048]{1,0:T(8,128)S(1)}, f32[136,2048]{1,0:T(8,128)S(1)}, u32[]{:S(2)}, u32[]{:S(2)}) collective-permute-start(f32[136,2048]{1,0:T(8,128)S(1)} %get-tuple-element.50), channel_id=1, source_target_pairs={{4,0},{8,4},{12,8},{5,1},{9,5},{13,9},{6,2},{10,6},{14,10},{7,3},{... | collective-permute-start | bytes 3342344 | tf_op jit(solution)/shard_map/ppermute | solution.py:26
  54.5 52.6 %collective-permute-start.2 = (f32[136,2048]{1,0:T(8,128)S(1)}, f32[136,2048]{1,0:T(8,128)}, u32[]{:S(2)}, u32[]{:S(2)}) collective-permute-start(f32[136,2048]{1,0:T(8,128)S(1)} %get-tuple-element.49), channel_id=1, source_target_pairs={{0,8},{4,12},{1,9},{5,13},{2,10},{6,14},{3,11},{7,15},{16,24},{20,... | collective-permute-start | bytes 3342344 | tf_op jit(solution)/shard_map/ppermute | solution.py:26
  61.0 31.7 %collective-permute-start.1 = (f32[136,2048]{1,0:T(8,128)S(1)}, f32[136,2048]{1,0:T(8,128)S(1)}, u32[]{:S(2)}, u32[]{:S(2)}) collective-permute-start(f32[136,2048]{1,0:T(8,128)S(1)} %get-tuple-element.49), channel_id=1, source_target_pairs={{0,4},{4,8},{8,12},{1,5},{5,9},{9,13},{2,6},{6,10},{10,14},{3,7},{... | collective-permute-start | bytes 3342344 | tf_op jit(solution)/shard_map/ppermute | solution.py:26
  108.9 23.4 %copy-start.9 = (f32[512,256]{1,0:T(8,128)S(1)}, f32[512,256]{1,0:T(8,128)}, u32[]{:S(2)}) copy-start(f32[512,256]{1,0:T(8,128)} %copy-done.8) | copy-start | bytes 1572868
  108.9 23.4 %copy-start.10 = (f32[512,256]{1,0:T(8,128)S(1)}, f32[512,256]{1,0:T(8,128)}, u32[]{:S(2)}) copy-start(f32[512,256]{1,0:T(8,128)} %get-tuple-element.84) | copy-start | bytes 1572868
  108.9 23.4 %copy-start.11 = (bf16[1,512,256]{2,1,0:T(8,128)(2,1)S(1)}, bf16[1,512,256]{2,1,0:T(8,128)(2,1)}, u32[]{:S(2)}) copy-start(bf16[1,512,256]{2,1,0:T(8,128)(2,1)} %param.15) | copy-start | bytes 786436
  108.9 23.4 %copy-start.15 = (f32[512]{0:T(512)S(1)}, f32[512]{0:T(512)}, u32[]{:S(2)}) copy-start(f32[512]{0:T(512)} %copy-done.14) | copy-start | bytes 6148
  135.5 5.9 %collective-permute-start.5 = (f32[3,2304]{1,0:T(4,128)S(1)}, f32[3,2304]{1,0:T(4,128)S(1)}, u32[]{:S(2)}, u32[]{:S(2)}) collective-permute-start(f32[3,2304]{1,0:T(4,128)S(1)} %pad_maximum_fusion.3), channel_id=1, source_target_pairs={{4,0},{8,4},{12,8},{5,1},{9,5},{13,9},{6,2},{10,6},{14,10},{7,3},{... | collective-permute-start | bytes 82952 | tf_op jit(solution)/shard_map/ppermute | solution.py:26
  (13 other events, 12.2 us)

commit v3 on v2

--- a/solution.py
+++ b/solution.py
@@ -81,38 +81,102 @@
     return 1.0 / (1.0 + jnp.exp(-value))
 
 
-def states_kernel(x, rim, dy, taps, usable, cols, write_t, read_t, keep, pre_out, fresh, back, pad, wt_s, rt_s):
+def start_kernel(
+    reach, x, rim, dy, taps, usable, cols, projected, keep, rows_ref, gram, gram_t,
+    pre_out, y_out, u_out, dgram, entering, leaving, closing,
+    pad, wt_s, rt_s, g_s, gt_s, xs_s, fresh, back, got, send_sem, recv_sem,
+):
+    phase, g = pl.program_id(0), pl.program_id(1)
+    pairs = pl.num_programs(1)
+    ctx, count = lax.axis_index("ctx"), lax.axis_size("ctx")
     rows = x.shape[0]
 
-    @pl.when(pl.program_id(0) == 0)
+    def each_copy(pair, act_sent, act_got):
+        for j in range(1, reach + 1):
+            for way, (source, step) in enumerate(((fresh, j), (back, -j))):
+                to, origin = ctx + step, ctx - step
+                copy = pltpu.make_async_remote_copy(
+                    src_ref=source.at[pair],
+                    dst_ref=got.at[way, j - 1, pair],
+                    send_sem=send_sem.at[way, j - 1, pair],
+                    recv_sem=recv_sem.at[way, j - 1, pair],
+                    device_id={"ctx": to},
+                    device_id_type=pl.DeviceIdType.MESH,
+                )
+                pl.when((to >= 0) & (to < count))(partial(act_sent, copy))
+                pl.when((origin >= 0) & (origin < count))(partial(act_got, copy))
+
+    @pl.when((phase == 0) & (g == 0))
     def _():
-        wt_s[0], wt_s[1] = split(write_t[...])
-        rt_s[0], rt_s[1] = split(read_t[...])
-
-    pad[0:8] = rim[...]
-    pad[8 : 8 + rows] = x[...].astype(f32)
-    pre = jnp.zeros((rows, LANES), f32)
-    for k in range(KERNEL):
-        term = taps[k : k + 1, :] * pad[5 + k : 5 + k + rows]
-        if k < KERNEL - 1:
-            term = term * usable[:, k * LANES : (k + 1) * LANES]
-        pre = pre + term
-    pre_out[...] = pre
-    columns = cols[0]
-    weighted = pre * sigmoid(pre) * (spread(columns, C_STEP) * spread(columns, C_LEAVE))
-    fresh[:STATE] = mm3((wt_s[0], wt_s[1]), split(weighted))
-    fresh[STATE:] = jnp.broadcast_to(keep[...], (8, LANES))
-    grad = dy[...].astype(f32) * spread(columns, C_ENTER)
-    back[:STATE] = mm3((rt_s[0], rt_s[1]), split(grad))
-    back[STATE:] = jnp.broadcast_to(keep[...], (8, LANES))
-
-
-def local_kernel(pre_ref, dy, cols, rows_ref, gram, gram_t, y_out, u_out, dgram, g_s, gt_s):
+        barrier = pltpu.get_barrier_semaphore()
+        for o in range(1, count):
+            pl.semaphore_signal(
+                barrier, inc=1, device_id={"ctx": lax.rem(ctx + o, count)}, device_id_type=pl.DeviceIdType.MESH
+            )
+        pl.semaphore_wait(barrier, count - 1)
+
+        for j in range(1, reach + 1):
+            for way, origin in enumerate((ctx - j, ctx + j)):
+
+                @pl.when((origin < 0) | (origin >= count))
+                def _():
+                    got[way, j - 1] = jnp.zeros(got.shape[2:], f32)
+
+        wt_s[0], wt_s[1] = split(projected[:, :STATE].T)
+        rt_s[0], rt_s[1] = split(projected[:, STATE:].T)
+
+    @pl.when(phase == 0)
+    def _():
+        pad[0:8] = rim[...]
+        pad[8 : 8 + rows] = x[...].astype(f32)
+        pre = jnp.zeros((rows, LANES), f32)
+        for k in range(KERNEL):
+            term = taps[k : k + 1, :] * pad[5 + k : 5 + k + rows]
+            if k < KERNEL - 1:
+                term = term * usable[:, k * LANES : (k + 1) * LANES]
+            pre = pre + term
+        pre_out[...] = pre
+        columns = cols[0]
+        xs = pre * sigmoid(pre) * spread(columns, C_STEP)
+        xs_s[g] = xs
+        fresh[g, :STATE] = mm3((wt_s[0], wt_s[1]), split(xs * spread(columns, C_LEAVE)))
+        fresh[g, STATE:] = jnp.broadcast_to(keep[...], (8, LANES))
+        grad = dy[...].astype(f32) * spread(columns, C_ENTER)
+        back[g, :STATE] = mm3((rt_s[0], rt_s[1]), split(grad))
+        back[g, STATE:] = jnp.broadcast_to(keep[...], (8, LANES))
+        each_copy(g, lambda copy: copy.start(), lambda copy: None)
+
+    @pl.when(phase == 1)
+    def _():
+        local_part(g, xs_s[g], dy, cols, rows_ref, gram, gram_t, y_out, u_out, dgram, g_s, gt_s)
+
+    @pl.when((phase == 1) & (g == pairs - 1))
+    def _():
+        def join(pair, carry):
+            each_copy(pair, lambda copy: copy.wait_send(), lambda copy: copy.wait_recv())
+            sums = []
+            for way in range(2):
+                total = got[way, 0, pair, :STATE]
+                decay = got[way, 0, pair, STATE : STATE + 1]
+                for j in range(1, reach):
+                    total = total + decay * got[way, j, pair, :STATE]
+                    decay = decay * got[way, j, pair, STATE : STATE + 1]
+                sums.append(total)
+            entering[pair] = sums[0]
+            leaving[pair] = sums[1]
+            ending = fresh[pair, STATE : STATE + 1] * sums[0] + fresh[pair, :STATE]
+            closing[pair] = jnp.sum(sums[1] * ending, axis=0, keepdims=True)
+            return carry
+
+        lax.fori_loop(0, pairs, join, 0)
+
+
+def local_part(g, xs, dy, cols, rows_ref, gram, gram_t, y_out, u_out, dgram, g_s, gt_s):
     rows = dy.shape[0]
     blocks = rows // SUB
     half = rows // 2
 
-    @pl.when(pl.program_id(0) == 0)
+    @pl.when(g == 0)
     def _():
         dgram[...] = jnp.zeros_like(dgram)
         g_s[0], g_s[1] = split(gram[...])
@@ -121,8 +185,6 @@
     columns = cols[0]
     lanes = first_lanes(SUB)
     zero = jnp.zeros((SUB, LANES), f32)
-    pre = pre_ref[...]
-    xs = pre * sigmoid(pre) * spread(columns, C_STEP)
     grad = dy[...].astype(f32)
     for b in range(blocks):
         at = slice(b * SUB, (b + 1) * SUB)
@@ -191,8 +253,8 @@
     values = pre * gate
     step = spread(columns, C_STEP)
     grad = dy[...].astype(f32)
-    ent = split(entering[...])
-    lea = split(leaving[...])
+    ent = split(entering[0])
+    lea = split(leaving[0])
     enter = spread(columns, C_ENTER)
     leave = spread(columns, C_LEAVE)
     y = y_in[...] + enter * mm3(read, ent)
@@ -341,7 +403,6 @@
     decay_log,
     skip_gain,
     out_grad,
-    interpret=False,
 ):
     rows, channels = value_input.shape[1:]
     heads = step_raw.shape[1]
@@ -415,9 +476,7 @@
     cols_spec = pl.BlockSpec((1, rows, 6 * PAIR), lambda g: (g, 0, 0))
     eight_spec = pl.BlockSpec((8, LANES), lambda g: (0, g))
     taps_spec = pl.BlockSpec((KERNEL, LANES), lambda g: (0, g))
-    one_spec = pl.BlockSpec((1, LANES), lambda g: (0, g))
-    sent_spec = pl.BlockSpec((STATE + 8, LANES), lambda g: (0, g))
-    state_spec = pl.BlockSpec((STATE, LANES), lambda g: (0, g))
+    state_spec = pl.BlockSpec((1, STATE, LANES), lambda g: (g, 0, 0))
 
     def wide(value):
         return jnp.repeat(value, HEAD_DIM)[None, :]
@@ -431,42 +490,42 @@
     params = pltpu.CompilerParams(
         dimension_semantics=("arbitrary",), vmem_limit_bytes=48 * 1024 * 1024
     )
-    pre, fresh, back = pl.pallas_call(
-        states_kernel,
-        grid=(pairs,),
-        in_specs=[col_spec, eight_spec, col_spec, taps_spec, fixed(rows, rim * LANES), cols_spec,
-                  fixed(STATE, rows), fixed(STATE, rows), one_spec],
-        out_specs=[col_spec, sent_spec, sent_spec],
-        out_shape=[like(rows, channels), like(STATE + 8, channels), like(STATE + 8, channels)],
-        scratch_shapes=[pltpu.VMEM((rows + 8, LANES), f32), pltpu.VMEM((2, STATE, rows), bf16),
-                        pltpu.VMEM((2, STATE, rows), bf16)],
-        compiler_params=params,
-        interpret=interpret,
-        name="states",
-    )(x, value_rim, dy, conv_value, usable_wide, cols, write_rows.T, read_rows.T, wide(keep))
-
-    entering, leaving = jnp.zeros((2, STATE, channels), f32)
-    ahead_keep, behind_keep = jnp.ones((2, 1, channels), f32)
-    for j in range(1, reach + 1):
-        ahead, behind = shifted(fresh, "ctx", j), shifted(back, "ctx", -j)
-        entering = entering + ahead_keep * ahead[:STATE]
-        leaving = leaving + behind_keep * behind[:STATE]
-        ahead_keep = ahead_keep * ahead[STATE : STATE + 1]
-        behind_keep = behind_keep * behind[STATE : STATE + 1]
-
-    y_local, u_local, dgram = pl.pallas_call(
-        local_kernel,
-        grid=(pairs,),
-        in_specs=[col_spec, col_spec, cols_spec, pl.BlockSpec((1, PAIR, rows), lambda g: (g, 0, 0)),
-                  fixed(rows, rows), fixed(rows, rows)],
-        out_specs=[col_spec, col_spec, fixed(rows, rows)],
-        out_shape=[like(rows, channels), like(rows, channels), like(rows, rows)],
-        scratch_shapes=[pltpu.VMEM((2, rows, rows), bf16), pltpu.VMEM((2, rows, rows), bf16)],
-        compiler_params=params,
-        cost_estimate=pl.CostEstimate(flops=30 * 10**9, bytes_accessed=20 * 10**6, transcendentals=10**7),
-        interpret=interpret,
-        name="local",
-    )(pre, dy, cols, row_form, gram, gram_t)
+    def early(*shape):
+        return pl.BlockSpec(shape, lambda p, g: (0, jnp.where(p == 0, g, pairs - 1)))
+
+    def late(*shape):
+        return pl.BlockSpec(shape, lambda p, g: (0, jnp.where(p == 0, 0, g)))
+
+    def always(*shape):
+        return pl.BlockSpec(shape, lambda p, g: (0,) * len(shape))
+
+    sent = (STATE + 8, LANES)
+    pre, y_local, u_local, dgram, entering, leaving, closing = pl.pallas_call(
+        partial(start_kernel, reach),
+        grid=(2, pairs),
+        in_specs=[early(rows, LANES), early(8, LANES), pl.BlockSpec((rows, LANES), lambda p, g: (0, g)),
+                  early(KERNEL, LANES), always(rows, rim * LANES),
+                  pl.BlockSpec((1, rows, 6 * PAIR), lambda p, g: (g, 0, 0)), always(rows, 2 * STATE),
+                  early(1, LANES), pl.BlockSpec((1, PAIR, rows), lambda p, g: (g, 0, 0)),
+                  always(rows, rows), always(rows, rows)],
+        out_specs=[early(rows, LANES), late(rows, LANES), late(rows, LANES), always(rows, rows),
+                   always(pairs, STATE, LANES), always(pairs, STATE, LANES), always(pairs, 1, LANES)],
+        out_shape=[like(rows, channels), like(rows, channels), like(rows, channels), like(rows, rows),
+                   like(pairs, STATE, LANES), like(pairs, STATE, LANES), like(pairs, 1, LANES)],
+        scratch_shapes=[
+            pltpu.VMEM((rows + 8, LANES), f32), pltpu.VMEM((2, STATE, rows), bf16),
+            pltpu.VMEM((2, STATE, rows), bf16), pltpu.VMEM((2, rows, rows), bf16),
+            pltpu.VMEM((2, rows, rows), bf16), pltpu.VMEM((pairs, rows, LANES), f32),
+            pltpu.VMEM((pairs, *sent), f32), pltpu.VMEM((pairs, *sent), f32),
+            pltpu.VMEM((2, reach, pairs, *sent), f32),
+            pltpu.SemaphoreType.DMA((2, reach, pairs)), pltpu.SemaphoreType.DMA((2, reach, pairs)),
+        ],
+        compiler_params=pltpu.CompilerParams(
+            dimension_semantics=("arbitrary", "arbitrary"), vmem_limit_bytes=52 * 1024 * 1024,
+            collective_id=1, has_side_effects=True,
+        ),
+        name="start",
+    )(x, value_rim, dy, conv_value, usable_wide, cols, projected, wide(keep), row_form, gram, gram_t)
 
     mixed, vgrad, tail, rim_grad, tap_grad, token_sums, skip_sums, dproj = pl.pallas_call(
         final_kernel,
@@ -483,7 +542,6 @@
         scratch_shapes=[pltpu.VMEM((rows + 8, LANES), f32), pltpu.VMEM((rows + 16, LANES), f32),
                         pltpu.VMEM((2, rows, 2 * STATE), bf16)],
         compiler_params=params,
-        interpret=interpret,
         name="final",
     )(pre, x, value_rim, dy, cols, usable_wide, conv_value, wide(skip_gain), projected, entering, leaving,
       y_local, u_local)
@@ -497,7 +555,6 @@
     sums = token_sums.reshape(pairs, 2, PAIR, rows)
     out_dot = sums[:, 0].reshape(heads, rows)
     in_dot = sums[:, 1].reshape(heads, rows)
-    closing = jnp.sum(leaving * (wide(keep) * entering + fresh[:STATE]), axis=0)
     closing = jnp.sum(closing.reshape(heads, HEAD_DIM), axis=1)
     dcum = out_dot - step * in_dot
     order = jnp.arange(rows)
@@ -533,9 +590,9 @@
     )
 
 
-def solution(mesh, interpret=False):
+def solution(mesh):
     return jax.shard_map(
-        partial(on_device, interpret=interpret),
+        on_device,
         mesh=mesh,
         in_specs=(
             P("dp", "ctx", "head"),

time: 171 us -> 149 us (0.87)
  Pallas kernels: 88 us -> 103 us
  waiting for transfers between devices: 18.9 us -> 4.5 us
  starting transfers between devices: 19.2 us -> 6.14 us
  local copies, waits for them, and re-layouts: 20.2 us -> 11.5 us
  other arithmetic: 11.6 us -> 8.49 us
  matrix products: 9.18 us -> 11.8 us
    pallas_call x2 -> x1, Pallas kernels: 42.1 us -> 57.6 us  [on_device(): pl.pallas_call(partial(start_kernel, reach), grid=(2, pairs), in_specs=[e...]
    ppermute x6 -> x2, waiting for transfers between devices: 18.9 us -> 4.5 us  [shifted(): lax.ppermute(value, axis, [(source, source + steps) for source in range(l...]
    ppermute x6 -> x2, starting transfers between devices: 19.2 us -> 6.14 us  [shifted(): lax.ppermute(value, axis, [(source, source + steps) for source in range(l...]
    transpose x3 -> x0, local copies, waits for them, and re-layouts: 4.38 us -> none  [on_device(): pre, fresh, back = pl.pallas_call(states_kernel, grid=(pairs,), in_specs=...]
    unnamed x65 -> x19, local copies, waits for them, and re-layouts: 3.97 us -> 0.77 us
    reduce_sum x1 -> x0, other arithmetic: 1.75 us -> none  [on_device(): closing = jnp.sum(leaving * (wide(keep) * entering + fresh[:STATE]), axis=0)]
  transfers between devices with their start and end apart: 6 -> 2, of which waited for: 2 -> 1; matrix products, arithmetic and copies ran while one was open for 10% -> 8% of each run, Pallas kernels for 15% -> 0%
where the time goes in v3:
time: 149 us; the launch traced here: 147 us
  Pallas kernels  103 us (69%)
  matrix products  11.8 us (8%)
  local copies, waits for them, and re-layouts  11.5 us (8%)
  other arithmetic  8.49 us (6%)
  starting transfers between devices  6.14 us (4%)
  waiting for transfers between devices  4.5 us (3%)
  between operations  1.82 us (1%)
    pallas_call x1, Pallas kernels, on_device(): pl.pallas_call(partial(start_kernel, reach), grid=(2, pairs), in_specs=[e...  57.6 us
    pallas_call x1, Pallas kernels, on_device(): pl.pallas_call(final_kernel, grid=(pairs,), in_specs=[col_spec, col_spec,...  23 us
    pallas_call x1, Pallas kernels, sum_across(): pl.pallas_call(partial(sum_kernel, groups, members, local_rows), in_specs...  22.3 us
    ppermute x2, starting transfers between devices, shifted(): lax.ppermute(value, axis, [(source, source + steps) for source in range(l...  6.14 us
    ppermute x2, waiting for transfers between devices, shifted(): lax.ppermute(value, axis, [(source, source + steps) for source in range(l...  4.5 us
    dot_general x1, matrix products, on_device(): dwrite = jnp.dot(dgram.T, read_rows, precision=precise)  3.2 us
  transfers between devices with their start and end apart: 2, of which 1 were waited for; matrix products, arithmetic and copies ran while one was open for 8% of the time, Pallas kernels for 0%

profile of v3, /device:TPU:0, one launch (start us, length us, event | category | flops | bytes accessed | tf_op | source)
XLA Modules:
  0.0 147.1 jit_solution(6606590280676050366)
XLA Ops:
  0.6 0.8 slice_bitcast_fusion
  1.4 0.7 slice_bitcast_fusion.1
  2.1 4.8 %collective-permute-start = (bf16[3,2304]{1,0:T(4,128)(2,1)S(1)}, bf16[3,2304]{1,0:T(4,128)(2,1)S(1)}, u32[]{:S(2)}, u32[]{:S(2)}) collective-permute-start(bf16[3,2304]{1,0:T(4,128)(2,1)S(1)} %pad_maximum_fusion.4), channel_id=1, source_target_pairs={{0,4},{4,8},{8,12},{1,5},{5,9},{9,13},{2,6},{6,10},{10,14},{3,7},{... | collective-permute-start | bytes 41480 | tf_op jit(solution)/shard_map/ppermute | solution.py:26
  7.0 0.7 fusion.62
  7.6 0.9 squeeze.25
  8.5 0.9 broadcast_multiply_fusion
  9.6 1.0 compare_select_fusion.1
  10.6 0.8 reduce-window.8
  11.4 0.7 select_reduce_fusion
  13.4 0.7 fusion.47
  14.1 1.0 bitcast_convert_fusion
  17.1 2.7 %copy.52.cols = f32[16,512,12]{2,1,0:T(8,128)} copy(f32[16,512,12]{1,0,2:T(8,128)S(1)} %bitcast.93) | data formatting | bytes 786432 | tf_op jit(solution)/shard_map/reshape | solution.py:472
  20.5 2.0 %convolution_select_fusion.gram_t = f32[512,512]{1,0:T(8,128)} fusion(s32[512]{0:T(512)S(1)} %select_reduce_fusion, s32[512]{0:T(512)S(1)} %iota_add_fusion, f32[512,256]{1,0:T(8,128)S(1)} %get-tuple-element.82.projected), kind=kOutput, calls=%fused_computation | convolution fusion | flops 403701760 | bytes 1579008 | tf_op jit(solution)/shard_map/dot_general | solution.py:438
  22.6 2.0 %convolution_select_fusion.1.gram = f32[512,512]{1,0:T(8,128)} fusion(s32[512]{0:T(512)S(1)} %iota_add_fusion, s32[512]{0:T(512)S(1)} %select_reduce_fusion, f32[512,256]{1,0:T(8,128)S(1)} %get-tuple-element.82.projected), kind=kOutput, calls=%fused_computation.1 | convolution fusion | flops 403701760 | bytes 1579008 | tf_op jit(solution)/shard_map/dot_general | solution.py:437
  24.6 57.6 %start.1 = (f32[512,2048]{1,0:T(8,128)}, f32[512,2048]{1,0:T(8,128)}, f32[512,2048]{1,0:T(8,128)}, f32[512,512]{1,0:T(8,128)}, f32[16,128,128]{2,1,0:T(8,128)}, ...) custom-call(bf16[512,2048]{1,0:T(8,128)(2,1)} %bitcast.89, f32[8,2048]{1,0:T(8,128)S(1)} %pad_convert_fusion.rim, ...), custom_call_target="tpu_custom_call" | custom-call | tf_op jit(solution)/shard_map/start/pallas_call | solution.py:503
  82.3 2.5 %fusion = f32[512,128]{1,0:T(8,128)S(1)} fusion(f32[512,512]{1,0:T(8,128)} %get-tuple-element.59, s32[512]{0:T(512)S(1)} %iota_add_fusion, s32[512]{0:T(512)S(1)} %select_reduce_fusion, f32[512,256]{1,0:T(8,128)S(1)} %get-tuple-element.82.projected), kind=kOutput, calls=%fused_computation.5 | convolution fusion | flops 403701760 | bytes 1579008 | tf_op jit(solution)/shard_map/dot_general | solution.py:550
  84.7 3.2 %fusion.2 = f32[512,128]{1,0:T(8,128)S(1)} fusion(f32[512,512]{1,0:T(8,128)} %get-tuple-element.59, s32[512]{0:T(512)S(1)} %iota_add_fusion, s32[512]{0:T(512)S(1)} %select_reduce_fusion, f32[512,256]{1,0:T(8,128)S(1)} %get-tuple-element.82.projected), kind=kOutput, calls=%fused_computation.7 | convolution fusion | flops 403701760 | bytes 1579008 | tf_op jit(solution)/shard_map/dot_general | solution.py:551
  88.0 23.0 %final.1 = (bf16[512,2048]{1,0:T(8,128)(2,1)}, bf16[512,2048]{1,0:T(8,128)(2,1)}, f32[8,2048]{1,0:T(8,128)S(1)}, f32[8,2048]{1,0:T(8,128)S(1)}, f32[4,2048]{1,0:...) custom-call(f32[512,2048]{1,0:T(8,128)} %get-tuple-element.49.pre_ref, ...), custom_call_target="tpu_custom_call" | custom-call | tf_op jit(solution)/shard_map/final/pallas_call | solution.py:530
  112.8 0.7 reduce.45
  113.9 1.1 fusion.57
  115.3 1.3 collective-permute-start.1
  116.6 4.5 %collective-permute-done.1 = f32[3,2304]{1,0:T(4,128)S(1)} collective-permute-done((f32[3,2304]{1,0:T(4,128)S(1)}, f32[3,2304]{1,0:T(4,128)S(1)}, u32[]{:S(2)}, u32[]{:S(2)}) %collective-permute-start.1) | collective-permute-done | bytes 27680 | tf_op jit(solution)/shard_map/ppermute | solution.py:26
  121.3 22.3 %sums.1 = (bf16[512,256]{1,0:T(8,128)(2,1)S(1)}, f32[72,128]{1,0:T(8,128)S(1)}, f32[8,128]{1,0:T(8,128)S(1)}) custom-call(f32[512,256]{1,0:T(8,128)S(1)} %scatter-add.9.part, f32[80,128]{1,0:T(8,128)S(1)} %pad_maximum_fusion.2.small), custom_call_target="tpu_custom_call" | custom-call | tf_op jit(solution)/shard_map/sums/pallas_call | solution.py:373
  146.4 0.7 copy.73
  (92 shorter events, 8.8 us)
Async XLA Ops:
  0.6 15.4 %copy-start.5 = (f32[4,256]{1,0:T(4,128)S(1)}, f32[4,256]{1,0:T(4,128)}, u32[]{:S(2)}) copy-start(f32[4,256]{1,0:T(4,128)} %param.19) | copy-start | bytes 12292
  2.1 18.0 %collective-permute-start = (bf16[3,2304]{1,0:T(4,128)(2,1)S(1)}, bf16[3,2304]{1,0:T(4,128)(2,1)S(1)}, u32[]{:S(2)}, u32[]{:S(2)}) collective-permute-start(bf16[3,2304]{1,0:T(4,128)(2,1)S(1)} %pad_maximum_fusion.4), channel_id=1, source_target_pairs={{0,4},{4,8},{8,12},{1,5},{5,9},{9,13},{2,6},{6,10},{10,14},{3,7},{... | collective-permute-start | bytes 41480 | tf_op jit(solution)/shard_map/ppermute | solution.py:26
  17.1 2.8 %copy-start.7 = (f32[32]{0:T(128)S(1)}, f32[32]{0:T(128)}, u32[]{:S(2)}) copy-start(f32[32]{0:T(128)} %param.22) | copy-start | bytes 388
  20.1 4.5 %copy-start.2 = (f32[4,2048]{1,0:T(4,128)S(1)}, f32[4,2048]{1,0:T(4,128)}, u32[]{:S(2)}) copy-start(f32[4,2048]{1,0:T(4,128)} %taps.3) | copy-start | bytes 98308
  82.2 5.7 %copy-start = (f32[16,128,128]{2,1,0:T(8,128)S(1)}, f32[16,128,128]{2,1,0:T(8,128)}, u32[]{:S(2)}) copy-start(f32[16,128,128]{2,1,0:T(8,128)} %get-tuple-element.50.entering) | copy-start | bytes 3145732
  82.2 5.7 %copy-start.1 = (f32[16,128,128]{2,1,0:T(8,128)S(1)}, f32[16,128,128]{2,1,0:T(8,128)}, u32[]{:S(2)}) copy-start(f32[16,128,128]{2,1,0:T(8,128)} %get-tuple-element.51.leaving) | copy-start | bytes 3145732
  87.9 23.0 %copy-start.3 = (bf16[1,512,256]{2,1,0:T(8,128)(2,1)S(1)}, bf16[1,512,256]{2,1,0:T(8,128)(2,1)}, u32[]{:S(2)}) copy-start(bf16[1,512,256]{2,1,0:T(8,128)(2,1)} %param.15) | copy-start | bytes 786436
  111.9 2.0 %copy-start.4 = (f32[1,32,512]{2,1,0:T(8,128)S(1)}, f32[1,32,512]{2,1,0:T(8,128)}, u32[]{:S(2)}) copy-start(f32[1,32,512]{2,1,0:T(8,128)} %param.16) | copy-start | bytes 196612
  111.9 2.0 %copy-start.6 = (f32[32]{0:T(128)S(1)}, f32[32]{0:T(128)}, u32[]{:S(2)}) copy-start(f32[32]{0:T(128)} %param.20) | copy-start | bytes 388
  115.3 5.9 %collective-permute-start.1 = (f32[3,2304]{1,0:T(4,128)S(1)}, f32[3,2304]{1,0:T(4,128)S(1)}, u32[]{:S(2)}, u32[]{:S(2)}) collective-permute-start(f32[3,2304]{1,0:T(4,128)S(1)} %pad_maximum_fusion.3), channel_id=1, source_target_pairs={{4,0},{8,4},{12,8},{5,1},{9,5},{13,9},{6,2},{10,6},{14,10},{7,3},{... | collective-permute-start | bytes 82952 | tf_op jit(solution)/shard_map/ppermute | solution.py:26
